TPU v7x, 256 devices: a whole 4x4x8 slice. The times are simulated.
256 devices in a mesh: dp: 4 (over x), ep: 64 (over y, z, core).
Axes of the slice: x: 4, y: 4, z: 8, core: 2. Of those that a mesh axis runs over, the one named last changes fastest.
Arguments:
- tokens: bfloat16 [4, 2048, 2048], P('dp', 'ep'), may hold values from -12 to 12
- cotangent: bfloat16 [4, 2048, 2048], P('dp', 'ep'), may hold values from -6 to 6
- assign: int32 [4, 2048, 8], P('dp', 'ep'), may hold values from 0 to 63, as said below
- w_router: bfloat16 [2048, 64], replicated, may hold values from -0.125 to 0.125
- w_gate: bfloat16 [64, 2048, 768], P('ep'), may hold values from -0.125 to 0.125
- w_up: bfloat16 [64, 2048, 768], P('ep'), may hold values from -0.125 to 0.125
- w_down: bfloat16 [64, 2048, 768], P('ep'), may hold values from -0.21875 to 0.21875
Outputs:
- grad_tokens: bfloat16 [4, 2048, 2048], P('dp', 'ep')
- grad_router: float32 [2048, 64], replicated
- grad_gate: bfloat16 [64, 2048, 768], P('ep', 'dp')
- grad_up: bfloat16 [64, 2048, 768], P('ep', 'dp')
- grad_down: bfloat16 [64, 2048, 768], P('ep', 'dp')
Inputs may be any that keep to these rules, and one draw needn't show every extreme that they name: `assign`: each token names 8 different experts; the routes of the 32 tokens of one device name one expert at most 8 times, and in every draw one expert is named exactly 8 times by the routes of every device.
All inputs are finite; a program needn't handle non-finite values.
Results may differ from a plain program's by a relative error of at most 0.015.
Values may be sent and summed in bfloat16 or wider, within the bound.
A program may use at most 128 MiB of HBM per device.

v0:
```python
import jax
import jax.numpy as jnp
from jax import lax
from jax.sharding import PartitionSpec as P

ITERS = 3


cos_scale = 48.0
eps_norm = 1e-06
contract_first = (((0,), (0,)), ((), ()))
contract_last = (((1,), (1,)), ((), ()))


def logit_map(flat_tokens, router):
    inner_products = jnp.dot(flat_tokens, router, precision=lax.Precision.HIGHEST)
    token_norm = jnp.sqrt(jnp.sum(flat_tokens * flat_tokens, axis=1) + eps_norm)
    column_norm = jnp.sqrt(jnp.sum(router * router, axis=0) + eps_norm)
    return cos_scale * inner_products / (token_norm[:, None] * column_norm[None, :])


def expert_backward(expert_rows, expert_cotangent, rows_gate, gate_matrix, up_matrix, down_matrix):
    gate_linear = jnp.dot(expert_rows, gate_matrix, preferred_element_type=jnp.float32)
    up_linear = jnp.dot(expert_rows, up_matrix, preferred_element_type=jnp.float32)
    sigmoid_gate = jax.nn.sigmoid(gate_linear)
    activation = gate_linear * sigmoid_gate
    product = activation * up_linear
    hidden = product.astype(jnp.bfloat16)
    weighted = (rows_gate[:, None] * product).astype(jnp.bfloat16)
    raw_back = jnp.dot(expert_cotangent, down_matrix, preferred_element_type=jnp.float32)
    gate_grad = jnp.sum(raw_back * hidden.astype(jnp.float32), axis=1).astype(jnp.bfloat16)
    scaled_back = rows_gate[:, None] * raw_back
    up_delta = (scaled_back * activation).astype(jnp.bfloat16)
    gate_delta = (
        scaled_back * up_linear * sigmoid_gate * (1.0 + gate_linear * (1.0 - sigmoid_gate))
    ).astype(jnp.bfloat16)
    route_back = (
        lax.dot_general(gate_delta, gate_matrix, contract_last, preferred_element_type=jnp.float32)
        + lax.dot_general(up_delta, up_matrix, contract_last, preferred_element_type=jnp.float32)
    ).astype(jnp.bfloat16)
    return (gate_grad, route_back, gate_delta, up_delta, weighted)


def column_sums(values):
    return lax.psum(jnp.sum(values, axis=0), "ep")


def per_device(tokens, cotangent, assign, w_router, w_gate, w_up, w_down):
    local_tokens = tokens[0]
    local_cotangent = cotangent[0]
    route_ids = assign[0]
    token_count, per_token = route_ids.shape
    model_width = local_tokens.shape[1]
    experts = w_router.shape[1]
    slot_cap = min(token_count, 2 * token_count * per_token // experts)
    logits, logit_vjp = jax.vjp(
        logit_map, local_tokens.astype(jnp.float32), w_router.astype(jnp.float32)
    )
    kernel_start = jnp.exp(logits)
    kernel = kernel_start
    saved_steps = []
    for sweep_index in range(ITERS):
        column = column_sums(kernel)
        scaled = kernel / column[None, :]
        row_total = jnp.sum(scaled, axis=1, keepdims=True)
        kernel = scaled / row_total
        saved_steps.append((column, scaled, row_total, kernel))
    expert_ids = jnp.arange(experts, dtype=jnp.int32)
    onehot = (route_ids[:, :, None] == expert_ids).astype(jnp.float32)
    picked = jnp.sum(onehot * kernel[:, None, :], axis=2)
    picked_sum = jnp.sum(picked, axis=1, keepdims=True)
    gates = picked / picked_sum
    gate_half = gates.astype(jnp.bfloat16)
    flat_route = route_ids.reshape(-1)
    member = (flat_route[:, None] == expert_ids).astype(jnp.int32)
    earlier = jnp.cumsum(member, axis=0) - member
    slot_index = jnp.sum(earlier * member, axis=1)
    target = flat_route * slot_cap + slot_index
    route_slots = (
        jnp.arange(experts * slot_cap, dtype=jnp.int32)[:, None] == target[None, :]
    ).astype(jnp.bfloat16)
    token_slots = jnp.sum(route_slots.reshape(experts * slot_cap, token_count, per_token), axis=2)
    send_tokens = jnp.dot(token_slots, local_tokens, preferred_element_type=jnp.float32).astype(
        jnp.bfloat16
    )
    send_cotangent = jnp.dot(
        token_slots, local_cotangent, preferred_element_type=jnp.float32
    ).astype(jnp.bfloat16)
    send_gate = jnp.dot(
        route_slots, gate_half.reshape(-1), preferred_element_type=jnp.float32
    ).astype(jnp.bfloat16)
    recv_tokens, recv_cotangent, recv_gate = (
        lax.all_to_all(
            send_tokens.reshape(experts, slot_cap, model_width),
            "ep",
            split_axis=0,
            concat_axis=0,
            tiled=True,
        ),
        lax.all_to_all(
            send_cotangent.reshape(experts, slot_cap, model_width),
            "ep",
            split_axis=0,
            concat_axis=0,
            tiled=True,
        ),
        lax.all_to_all(
            send_gate.reshape(experts, slot_cap), "ep", split_axis=0, concat_axis=0, tiled=True
        ),
    )
    expert_rows = recv_tokens.reshape(-1, model_width)
    expert_cotangent = recv_cotangent.reshape(-1, model_width)
    rows_gate = recv_gate.reshape(-1).astype(jnp.float32)
    gate_grad, route_back, gate_delta, up_delta, weighted = expert_backward(
        expert_rows, expert_cotangent, rows_gate, w_gate[0], w_up[0], w_down[0]
    )
    back_rows, back_gate = (
        lax.all_to_all(
            route_back.reshape(experts, slot_cap, model_width),
            "ep",
            split_axis=0,
            concat_axis=0,
            tiled=True,
        ),
        lax.all_to_all(
            gate_grad.reshape(experts, slot_cap), "ep", split_axis=0, concat_axis=0, tiled=True
        ),
    )
    expert_back = lax.dot_general(
        token_slots,
        back_rows.reshape(-1, model_width),
        contract_first,
        preferred_element_type=jnp.float32,
    )
    route_grad = lax.dot_general(
        route_slots, back_gate.reshape(-1), contract_first, preferred_element_type=jnp.float32
    ).reshape(token_count, per_token)
    hidden_units = gate_delta.shape[1]
    summed = lax.psum_scatter(
        jnp.concatenate(
            [
                lax.dot_general(
                    expert_rows, gate_delta, contract_first, preferred_element_type=jnp.float32
                ),
                lax.dot_general(
                    expert_rows, up_delta, contract_first, preferred_element_type=jnp.float32
                ),
                lax.dot_general(
                    expert_cotangent, weighted, contract_first, preferred_element_type=jnp.float32
                ),
            ],
            axis=1,
        ).astype(jnp.bfloat16),
        "dp",
        scatter_dimension=0,
        tiled=True,
    ).astype(jnp.float32)
    grad_gate = summed[:, :hidden_units]
    grad_up = summed[:, hidden_units : 2 * hidden_units]
    grad_down = summed[:, 2 * hidden_units :]
    picked_grad = (route_grad - jnp.sum(route_grad * gates, axis=1, keepdims=True)) / picked_sum
    kernel_grad = jnp.sum(onehot * picked_grad[:, :, None], axis=1)
    for sweep_index in reversed(range(ITERS)):
        column, scaled, row_total, kernel_step = saved_steps[sweep_index]
        scaled_grad = (
            kernel_grad - jnp.sum(kernel_grad * kernel_step, axis=1, keepdims=True)
        ) / row_total
        moment = lax.psum(jnp.sum(scaled_grad * scaled, axis=0), "ep")
        kernel_grad = (scaled_grad - moment[None, :]) / column[None, :]
    logit_grad = kernel_grad * kernel_start
    router_back, router_part = logit_vjp(logit_grad)
    grad_router = lax.psum(router_part, ("dp", "ep"))
    grad_tokens = (expert_back + router_back).astype(jnp.bfloat16)[None]
    return (
        grad_tokens,
        grad_router,
        grad_gate.astype(jnp.bfloat16)[None],
        grad_up.astype(jnp.bfloat16)[None],
        grad_down.astype(jnp.bfloat16)[None],
    )


def solution(mesh):
    return jax.shard_map(
        per_device,
        mesh=mesh,
        in_specs=(
            P("dp", "ep", None),
            P("dp", "ep", None),
            P("dp", "ep", None),
            P(),
            P("ep", None, None),
            P("ep", None, None),
            P("ep", None, None),
        ),
        out_specs=(
            P("dp", "ep", None),
            P(),
            P("ep", "dp", None),
            P("ep", "dp", None),
            P("ep", "dp", None),
        ),
        check_vma=False,
    )
```

profile of v0, /device:TPU:1, one launch (start us, length us, event | category | flops | bytes accessed | tf_op | source)
XLA Modules:
  0.0 1250.7 jit_solution(17761611733418999477)
XLA Ops:
  15.1 128.3 %psum.49 = f32[64]{0:T(128)S(1)} all-reduce(f32[64]{0:T(128)S(1)} %get-tuple-element.33), channel_id=1, replica_groups=mesh['dp'=4,'ep'=64] {'ep'}, use_global_device_ids=true, to_apply=%region_7.0 | all-reduce | flops 64 | bytes 512 | tf_op jit(solution)/shard_map/psum | solution.py:45
  143.6 128.4 %psum.50 = f32[64]{0:T(128)S(1)} all-reduce(f32[64]{0:T(128)S(1)} %fusion.67), channel_id=1, replica_groups=mesh['dp'=4,'ep'=64] {'ep'}, use_global_device_ids=true, to_apply=%region_10.0 | all-reduce | flops 64 | bytes 512 | tf_op jit(solution)/shard_map/psum | solution.py:45
  272.3 124.0 %psum.51 = f32[64]{0:T(128)S(1)} all-reduce(f32[64]{0:T(128)S(1)} %fusion.73), channel_id=1, replica_groups=mesh['dp'=4,'ep'=64] {'ep'}, use_global_device_ids=true, to_apply=%region_13.0 | all-reduce | flops 64 | bytes 512 | tf_op jit(solution)/shard_map/psum | solution.py:45
  399.8 4.7 all-to-all-start
  407.8 6.0 all-to-all-done
  413.8 5.6 all-to-all-start.2
  421.5 49.2 %all-to-all-done.2 = bf16[64,8,2048]{2,1,0:T(8,128)(2,1)} async-done(((bf16[64,8,2048]{2,1,0:T(8,128)(2,1)}), bf16[64,8,2048]{2,1,0:T(8,128)(2,1)}, u32[]{:S(2)}, u32[]{:S(2)}) %all-to-all-start.2) | async-done | bytes 2097184 | tf_op jit(solution)/shard_map/all_to_all | solution.py:93
  470.7 6.0 all-to-all-start.1
  477.1 5.5 fusion.6
  482.6 4.6 fusion.2
  487.2 40.7 %all-to-all-done.1 = bf16[64,8,2048]{2,1,0:T(8,128)(2,1)} async-done(((bf16[64,8,2048]{2,1,0:T(8,128)(2,1)}), bf16[64,8,2048]{2,1,0:T(8,128)(2,1)}, u32[]{:S(2)}, u32[]{:S(2)}) %all-to-all-start.1) | async-done | bytes 2097184 | tf_op jit(solution)/shard_map/all_to_all | solution.py:100
  527.9 4.6 convolution_convert_fusion
  532.5 4.0 multiply_reduce_fusion
  536.5 4.0 convolution_convert_fusion.1
  540.6 3.4 convolution_convert_fusion.2
  544.0 4.5 pad_maximum_fusion
  549.2 6.0 all-to-all-start.4
  555.3 3.2 fusion
  558.5 3.1 fusion.14
  564.3 8.0 all-to-all-start.3
  581.8 154.8 %psum.52 = f32[64]{0:T(128)} all-reduce(f32[64]{0:T(128)} %multiply_reduce_fusion.7), channel_id=1, replica_groups=mesh['dp'=4,'ep'=64] {'ep'}, use_global_device_ids=true, to_apply=%region_22.23 | all-reduce | flops 64 | bytes 512 | tf_op jit(solution)/shard_map/psum | solution.py:168
  739.6 125.5 %psum.53 = f32[64]{0:T(128)} all-reduce(f32[64]{0:T(128)} %get-tuple-element.31), channel_id=1, replica_groups=mesh['dp'=4,'ep'=64] {'ep'}, use_global_device_ids=true, to_apply=%region_25.26 | all-reduce | flops 64 | bytes 512 | tf_op jit(solution)/shard_map/psum | solution.py:168
  867.8 124.7 %psum.54 = f32[64]{0:T(128)} all-reduce(f32[64]{0:T(128)} %multiply_reduce_fusion.3), channel_id=1, replica_groups=mesh['dp'=4,'ep'=64] {'ep'}, use_global_device_ids=true, to_apply=%region_28.29 | all-reduce | flops 64 | bytes 512 | tf_op jit(solution)/shard_map/psum | solution.py:168
  1011.6 229.9 %all-reduce.2.cloned.1.call-done = f32[2048,64]{0,1:T(8,128)} async-done(((f32[2048,64]{0,1:T(8,128)}), f32[2048,64]{0,1:T(8,128)}) %all-reduce.2.cloned.1.call-update) | async-done | bytes 524304 | tf_op jit(solution)/shard_map/psum | solution.py:172
  (134 shorter events, 56.2 us)
Async XLA Ops:
  8.0 474.6 %copy-start = (bf16[1,2048,768]{2,1,0:T(8,128)(2,1)S(1)}, bf16[1,2048,768]{2,1,0:T(8,128)(2,1)}, u32[]{:S(2)}) copy-start(bf16[1,2048,768]{2,1,0:T(8,128)(2,1)} %param.11) | copy-start | bytes 9437188
  8.9 404.9 %copy-start.3 = (s32[1,32,8]{2,1,0:T(8,128)}, s32[1,32,8]{2,1,0:T(8,128)S(1)}, u32[]{:S(2)}) copy-start(s32[1,32,8]{2,1,0:T(8,128)S(1)} %copy.33) | copy-start | bytes 3076
  11.6 3.5 copy-start.16
  143.4 261.4 %copy-start.10 = (f32[64]{0:T(128)}, f32[64]{0:T(128)S(1)}, u32[]{:S(2)}) copy-start(f32[64]{0:T(128)S(1)} %psum.49) | copy-start | bytes 772
  143.5 261.3 %copy-start.11 = (f32[32]{0:T(128)}, f32[32]{0:T(128)S(1)}, u32[]{:S(2)}) copy-start(f32[32]{0:T(128)S(1)} %fusion.65) | copy-start | bytes 388
  272.0 132.8 %copy-start.12 = (f32[64]{0:T(128)}, f32[64]{0:T(128)S(1)}, u32[]{:S(2)}) copy-start(f32[64]{0:T(128)S(1)} %psum.50) | copy-start | bytes 772
  272.2 132.6 %copy-start.13 = (f32[32]{0:T(128)}, f32[32]{0:T(128)S(1)}, u32[]{:S(2)}) copy-start(f32[32]{0:T(128)S(1)} %fusion.70) | copy-start | bytes 388
  397.6 7.2 copy-start.21
  399.8 14.0 %all-to-all-start = ((bf16[64,1,8]{2,1,0:T(2,128)(2,1)}), bf16[64,1,8]{2,1,0:T(2,128)(2,1)S(1)}, u32[]{:S(2)}, u32[]{:S(2)}) async-start(bf16[64,1,8]{2,1,0:T(2,128)(2,1)} %all_to_all.25), calls=%async_computation | async-start | bytes 65536 | tf_op jit(solution)/shard_map/all_to_all | solution.py:107
  404.9 14.5 %copy-start.4 = (bf16[512,32]{0,1:T(8,128)(2,1)}, bf16[512,32]{0,1:T(8,128)(2,1)S(1)}, u32[]{:S(2)}) copy-start(bf16[512,32]{0,1:T(8,128)(2,1)S(1)} %fusion.41) | copy-start | bytes 98308
  407.8 11.6 copy-start.9
  413.8 56.9 %all-to-all-start.2 = ((bf16[64,8,2048]{2,1,0:T(8,128)(2,1)}), bf16[64,8,2048]{2,1,0:T(8,128)(2,1)}, u32[]{:S(2)}, u32[]{:S(2)}) async-start(bf16[64,8,2048]{2,1,0:T(8,128)(2,1)} %fusion.13), calls=%async_computation.2 | async-start | bytes 4194304 | tf_op jit(solution)/shard_map/all_to_all | solution.py:93
  470.7 57.2 %all-to-all-start.1 = ((bf16[64,8,2048]{2,1,0:T(8,128)(2,1)}), bf16[64,8,2048]{2,1,0:T(8,128)(2,1)}, u32[]{:S(2)}, u32[]{:S(2)}) async-start(bf16[64,8,2048]{2,1,0:T(8,128)(2,1)} %fusion.12), calls=%async_computation.1 | async-start | bytes 4194304 | tf_op jit(solution)/shard_map/all_to_all | solution.py:100
  476.7 524.9 %reduce-scatter.2.cloned.1.call-start = ((), (), s32[]{:S(2)}) async-start(), calls=%async_computation.7 | async-start | bytes 11796480 | tf_op jit(solution)/shard_map/reduce_scatter | solution.py:139
  527.8 4.6 copy-start.27
  527.8 4.7 copy-start.32
  527.8 4.7 copy-start.33
  536.5 4.0 copy-start.29
  536.5 4.0 copy-start.31
  549.2 15.0 %all-to-all-start.4 = ((bf16[64,1,8]{2,1,0:T(2,128)(2,1)}), bf16[64,1,8]{2,1,0:T(2,128)(2,1)}, u32[]{:S(2)}, u32[]{:S(2)}) async-start(bf16[64,1,8]{2,1,0:T(2,128)(2,1)} %convert_element_type.108), calls=%async_computation.4 | async-start | bytes 65536 | tf_op jit(solution)/shard_map/all_to_all | solution.py:125
  561.6 433.7 %copy-start.1 = (bf16[2048,64]{0,1:T(8,128)(2,1)S(1)}, bf16[2048,64]{0,1:T(8,128)(2,1)}, u32[]{:S(2)}) copy-start(bf16[2048,64]{0,1:T(8,128)(2,1)} %param.10) | copy-start | bytes 786436
  561.6 433.7 %copy-start.2 = (bf16[1,32,2048]{2,1,0:T(8,128)(2,1)S(1)}, bf16[1,32,2048]{2,1,0:T(8,128)(2,1)}, u32[]{:S(2)}) copy-start(bf16[1,32,2048]{2,1,0:T(8,128)(2,1)} %param.7) | copy-start | bytes 393220
  564.3 434.2 %all-to-all-start.3 = ((bf16[64,8,2048]{2,1,0:T(8,128)(2,1)}), bf16[64,8,2048]{2,1,0:T(8,128)(2,1)}, u32[]{:S(2)}, u32[]{:S(2)}) async-start(bf16[64,8,2048]{2,1,0:T(8,128)(2,1)} %fusion.14), calls=%async_computation.3 | async-start | bytes 4194304 | tf_op jit(solution)/shard_map/all_to_all | solution.py:118
  572.2 669.2 %all-reduce.2.cloned.1.call-start = ((), (), s32[]{:S(2)}) async-start(), calls=%async_computation.6 | async-start | bytes 1048576 | tf_op jit(solution)/shard_map/psum | solution.py:172
  (17 other events, 25.9 us)
Sparse Core Ops, SparseCore 0:
  548.6 88.0 reduce-scatter.1
Sparse Core Ops, SparseCore 1:
  997.4 244.0 all-reduce.1
where the time goes:
time: 1250 us
  blocking collectives  786 us (63%)
  waiting for transfers between devices  328 us (26%)
  matrix products  45.9 us (4%)
  starting transfers between devices  30.5 us (2%)
  other arithmetic  24.4 us (2%)
  local copies, waits for them, and re-layouts  19.8 us (2%)
  between operations  16 us (1%)
    psum x3, blocking collectives, per_device(): moment = lax.psum(jnp.sum(scaled_grad * scaled, axis=0), 'ep')  405 us
    psum x3, blocking collectives, column_sums(): return lax.psum(jnp.sum(values, axis=0), 'ep')  381 us
    psum x1, waiting for transfers between devices, per_device(): grad_router = lax.psum(router_part, ('dp', 'ep'))  230 us
    all_to_all x1, waiting for transfers between devices, per_device(): lax.all_to_all(send_tokens.reshape(experts, slot_cap, model_width), 'ep',...  49.2 us
    all_to_all x1, waiting for transfers between devices, per_device(): lax.all_to_all(send_cotangent.reshape(experts, slot_cap, model_width), 'e...  40.7 us
  transfers between devices with their start and end apart: 7, of which 5 were waited for; matrix products, arithmetic and copies ran while one was open for 4% of the time, Pallas kernels for 0%

commit v1 on v0

v1 whole, which is shorter than its diff:
```python
import functools
import heapq

import jax
import jax.numpy as jnp
from jax import lax
from jax.experimental import pallas as pl
from jax.experimental.pallas import tpu as pltpu
from jax.sharding import PartitionSpec as P

ITERS = 3
SLOTS = 8
LANES = 128
GROUP = 256
MESH = pl.DeviceIdType.MESH
f32 = jnp.float32
bf16 = jnp.bfloat16

cos_scale = 48.0
eps_norm = 1e-06
contract_first = (((0,), (0,)), ((), ()))
contract_last = (((1,), (1,)), ((), ()))


def torus_of(ep):
    ny = 4
    return ny, ep // (2 * ny)


def gather_plan(ny, nz, unit_us=2.7, mate_us=0.5, hop_us=1.0):
    def half(part, side):
        return side if part is None else (part if part == side else -1)

    def spread(which, a, b, part):
        na, nb = (nz, ny) if which == 0 else (ny, nz)
        out = []

        def along(axis, n, at, signs):
            for sign in signs:
                last = abs(at) + 1 == n // 2
                piece = half(part, 0 if sign > 0 else 1) if last else part
                if piece != -1:
                    out.append((axis, sign, piece))

        def onward(at, n):
            if at == 0:
                return (1, -1)
            return ((1,) if at > 0 else (-1,)) if abs(at) < n // 2 else ()

        if b == 0:
            along(0, na, a, onward(a, na))
        along(1, nb, b, onward(b, nb))
        return out

    heap, order, free, steps, ids = [], 0, {}, [], 0
    for which in (0, 1):
        heapq.heappush(heap, (0.0, order, None, which, 0, 0, None))
        order += 1
    while heap:
        now, _, arrival, which, a, b, part = heapq.heappop(heap)
        dy, dz = (b, a) if which == 0 else (a, b)
        sends = []
        for axis, sign, piece in spread(which, a, b, part):
            link = "zy"[axis] if which == 0 else "yz"[axis]
            share = 1.0 if piece is None else 0.5
            end = max(now, free.get((link, sign), 0.0)) + unit_us * share
            free[(link, sign)] = end
            na, nb = (a + sign, b) if axis == 0 else (a, b + sign)
            heapq.heappush(heap, (end + hop_us, order, ids, which, na, nb, piece))
            sends.append((ids, which, dy, dz, part if piece is None else piece, link, sign))
            order += 1
            ids += 1
        sends.append((ids, which, dy, dz, part, "mate", 0))
        ids += 1
        steps.append((None if arrival is None else (arrival, which, dy, dz, part), sends))
    return steps, ids


def place(ep, ny, nz):
    me = lax.axis_index("ep")
    core = lax.rem(me, 2)
    chip = me // 2
    return me, core, chip // nz, lax.rem(chip, nz)


def at_ep(nz, y, z, core):
    return (y * nz + z) * 2 + core


def enter(peers):
    barrier = pltpu.get_barrier_semaphore()
    for peer in peers:
        pl.semaphore_signal(barrier, inc=1, device_id=peer, device_id_type=MESH)
    pl.semaphore_wait(barrier, len(peers))


def dispatch_kernel(
    ep,
    tok_ref,
    cot_ref,
    assign_ref,
    router_ref,
    rows_tok,
    rows_cot,
    rows_gate,
    pick_out,
    kernels_out,
    columns_out,
    totals_out,
    logits_out,
    marks_out,
    slice_out,
    tok_all,
    cot_all,
    meta,
    row_mask,
    row_gate,
    meta_send,
    meta_recv,
    send_sem,
    recv_sem,
):
    ny, nz = torus_of(ep)
    count, width = tok_ref.shape
    experts = router_ref.shape[1]
    groups = ep * count // GROUP
    per_group = GROUP // count
    dp = lax.axis_index("dp")
    me, core, y, z = place(ep, ny, nz)
    mate = (dp, at_ep(nz, y, z, 1 - core))
    z_peers = [(dp, at_ep(nz, y, lax.rem(z + k, nz), core)) for k in range(1, nz)]
    y_peers = [(dp, at_ep(nz, lax.rem(y + k, ny), z, core)) for k in range(1, ny)]
    enter([mate, *z_peers, *y_peers])

    local = tok_ref[...]
    router = router_ref[...]
    wide = local.astype(f32)
    inverse_token = 1.0 / jnp.sqrt(jnp.sum(wide * wide, axis=1, keepdims=True) + eps_norm)
    router_wide = router.astype(f32)
    column_norm = jnp.sqrt(jnp.sum(router_wide * router_wide, axis=0, keepdims=True) + eps_norm)
    inner = jnp.dot(local, router, preferred_element_type=f32)
    logits = cos_scale * inner * inverse_token / column_norm
    ids = lax.broadcasted_iota(jnp.int32, (count, experts), 1)
    routes = assign_ref[...]
    hit = jnp.zeros((count, experts), f32)
    for k in range(routes.shape[1]):
        hit = jnp.where(routes[:, k : k + 1] == ids, inverse_token, hit)
    mine = y * nz + z
    meta[core, mine] = jnp.concatenate([logits, hit], axis=1)
    tok_all[me] = local
    cot_all[me] = cot_ref[...]

    def meta_copy(n, part, peer):
        return pltpu.make_async_remote_copy(
            src_ref=part, dst_ref=part, send_sem=meta_send.at[n], recv_sem=meta_recv.at[n],
            device_id=peer, device_id_type=MESH,
        )

    def meta_part(c, block, blocks):
        return meta.at[c, pl.ds(block, blocks)]

    z_copies = [meta_copy(k, meta_part(core, mine, 1), p) for k, p in enumerate(z_peers)]
    for copy in z_copies:
        copy.start()

    steps, total = gather_plan(ny, nz)
    ends = {
        ("z", 1): (dp, at_ep(nz, y, lax.rem(z + 1, nz), core)),
        ("z", -1): (dp, at_ep(nz, y, lax.rem(z + nz - 1, nz), core)),
        ("y", 1): (dp, at_ep(nz, lax.rem(y + 1, ny), z, core)),
        ("y", -1): (dp, at_ep(nz, lax.rem(y + ny - 1, ny), z, core)),
        ("mate", 0): mate,
    }
    tables = (tok_all, cot_all)

    def view(which, dy, dz, part, c):
        block = at_ep(nz, lax.rem(y - dy + 2 * ny, ny), lax.rem(z - dz + 2 * nz, nz), c)
        first, rows = (0, count) if part is None else (part * (count // 2), count // 2)
        return tables[which].at[block, pl.ds(first, rows)]

    def block_copy(n, ref, end):
        return pltpu.make_async_remote_copy(
            src_ref=ref, dst_ref=ref, send_sem=send_sem.at[n], recv_sem=recv_sem.at[n],
            device_id=ends[end], device_id_type=MESH,
        )

    started, mate_arrivals = [], []

    def run(step):
        arrival, sends = step
        if arrival is not None:
            n, which, dy, dz, part = arrival
            block_copy(n, view(which, dy, dz, part, core), ("z", 1)).wait_recv()
        for n, which, dy, dz, part, link, sign in sends:
            copy = block_copy(n, view(which, dy, dz, part, core), (link, sign))
            copy.start()
            started.append(copy)
            if link == "mate":
                mate_arrivals.append((n, which, dy, dz, part))

    def balance():
        for g in range(groups):
            blocks = []
            for b in range(g * per_group, (g + 1) * per_group):
                blocks.append(meta[b % 2, b // 2])
            flipped = jnp.concatenate(blocks, axis=0).T
            logits_out[:, g * GROUP : (g + 1) * GROUP] = flipped[:experts]
            marks_out[:, g * GROUP : (g + 1) * GROUP] = flipped[experts:]
        kernels_out[0] = jnp.exp(logits_out[...])
        for s in range(ITERS):
            kernel = kernels_out[s]
            column = jnp.sum(kernel, axis=1, keepdims=True)
            scaled = kernel / column
            row = jnp.sum(scaled, axis=0, keepdims=True)
            kernels_out[s + 1] = scaled / row
            columns_out[s] = jnp.broadcast_to(column, (experts, LANES))
            totals_out[s : s + 1, :] = row
        member = marks_out[...] > 0.0
        picked = jnp.where(member, kernels_out[ITERS], 0.0)
        picked_sum = jnp.sum(picked, axis=0, keepdims=True)
        totals_out[ITERS : ITERS + 1, :] = picked_sum
        totals_out[ITERS + 1 :, :] = jnp.broadcast_to(
            jnp.max(marks_out[...], axis=0, keepdims=True),
            (totals_out.shape[0] - ITERS - 1, totals_out.shape[1]),
        )
        own = marks_out[pl.ds(me, 1), :] > 0.0
        gate = jnp.where(own, kernels_out[ITERS, pl.ds(me, 1), :], 0.0) / picked_sum
        row_mask[...] = own.astype(f32)
        row_gate[...] = gate.astype(bf16).astype(f32)

    first, second = len(steps) // 12, len(steps) // 6
    third, fourth = len(steps) // 4, len(steps) // 3
    y_copies, mate_copy = [], None
    for at, step in enumerate(steps):
        if at == first:
            for k, copy in enumerate(z_copies):
                block = y * nz + lax.rem(z - 1 - k + nz, nz)
                meta_copy(k, meta_part(core, block, 1), mate).wait_recv()
            y_copies = [
                meta_copy(nz - 1 + k, meta_part(core, y * nz, nz), p) for k, p in enumerate(y_peers)
            ]
            for copy in y_copies:
                copy.start()
        if at == second:
            for k in range(ny - 1):
                block = lax.rem(y - 1 - k + ny, ny) * nz
                meta_copy(nz - 1 + k, meta_part(core, block, nz), mate).wait_recv()
            mate_copy = meta_copy(nz + ny - 2, meta_part(core, 0, ny * nz), mate)
            mate_copy.start()
        if at == third:
            meta_copy(nz + ny - 2, meta_part(1 - core, 0, ny * nz), mate).wait_recv()
        if at == fourth:
            balance()
        run(step)
    for n, which, dy, dz, part in mate_arrivals:
        block_copy(n, view(which, dy, dz, part, 1 - core), ("mate", 0)).wait_recv()

    before = lax.broadcasted_iota(jnp.int32, (GROUP, GROUP), 0)
    after = lax.broadcasted_iota(jnp.int32, (GROUP, GROUP), 1)
    earlier = jnp.where((before < after) & (before // count == after // count), 1.0, 0.0).astype(bf16)
    slots = per_group * SLOTS
    slot_ids = lax.broadcasted_iota(jnp.int32, (slots, GROUP), 0).astype(f32)
    base = (lax.broadcasted_iota(jnp.int32, (1, GROUP), 1) // count * SLOTS).astype(f32)

    def compact(g, carry):
        lanes = pl.ds(pl.multiple_of(g * GROUP, GROUP), GROUP)
        rows = pl.ds(pl.multiple_of(g * slots, slots), slots)
        named = row_mask[:, lanes]
        rank = jnp.dot(
            jnp.broadcast_to(named, (8, GROUP)).astype(bf16), earlier, preferred_element_type=f32
        )[0:1]
        target = jnp.where(named > 0.0, base + rank, -1.0)
        chosen = jnp.where(slot_ids == target, 1.0, 0.0)
        rows_gate[rows, :] = jnp.sum(chosen * row_gate[:, lanes], axis=1, keepdims=True)
        pick = chosen.astype(bf16)
        pick_out[g] = pick
        blocks = pl.ds(g * per_group, per_group)
        rows_tok[rows, :] = jnp.dot(
            pick, tok_all[blocks].reshape(GROUP, width), preferred_element_type=f32
        ).astype(bf16)
        rows_cot[rows, :] = jnp.dot(
            pick, cot_all[blocks].reshape(GROUP, width), preferred_element_type=f32
        ).astype(bf16)
        return carry

    lax.fori_loop(0, groups, compact, 0)
    share = me // (ep // (width // LANES))
    slice_out[...] = tok_all[:, :, pl.ds(pl.multiple_of(share * LANES, LANES), LANES)]

    for copy in [*z_copies, *y_copies, mate_copy, *started]:
        copy.wait_send()


def dispatch(tokens, cotangent, assign, router, ep):
    ny, nz = torus_of(ep)
    count, width = tokens.shape
    experts = router.shape[1]
    total = ep * count
    groups = total // GROUP
    copies = gather_plan(ny, nz)[1]
    small = nz + ny - 1
    shape = jax.ShapeDtypeStruct
    vmem = pl.BlockSpec(memory_space=pltpu.VMEM)
    return pl.pallas_call(
        functools.partial(dispatch_kernel, ep),
        out_shape=(
            shape((ep * SLOTS, width), bf16),
            shape((ep * SLOTS, width), bf16),
            shape((ep * SLOTS, 1), f32),
            shape((groups, GROUP // count * SLOTS, GROUP), bf16),
            shape((ITERS + 1, experts, total), f32),
            shape((ITERS, experts, LANES), f32),
            shape((8, total), f32),
            shape((experts, total), f32),
            shape((experts, total), f32),
            shape((ep, count, LANES), bf16),
        ),
        in_specs=[vmem] * 4,
        out_specs=(vmem,) * 10,
        scratch_shapes=[
            pltpu.VMEM((ep, count, width), bf16),
            pltpu.VMEM((ep, count, width), bf16),
            pltpu.VMEM((2, ny * nz, count, 2 * experts), f32),
            pltpu.VMEM((1, total), f32),
            pltpu.VMEM((1, total), f32),
            pltpu.SemaphoreType.DMA((small,)),
            pltpu.SemaphoreType.DMA((small,)),
            pltpu.SemaphoreType.DMA((copies,)),
            pltpu.SemaphoreType.DMA((copies,)),
        ],
        compiler_params=pltpu.CompilerParams(
            collective_id=1, has_side_effects=True, vmem_limit_bytes=48 * 2**20
        ),
    )(tokens, cotangent, assign, router)


def split_three(value):
    high = value.astype(bf16)
    rest = value - high.astype(f32)
    middle = rest.astype(bf16)
    return high, middle, (rest - middle.astype(f32)).astype(bf16)


def router_kernel(
    ep,
    n_dp,
    grad_ref,
    pick_ref,
    kernels,
    columns,
    totals,
    logits_ref,
    marks_ref,
    slice_ref,
    tok_ref,
    router_ref,
    back_out,
    router_out,
    table,
    grad,
    spread,
    turned,
    parts,
    shares,
    sends,
    recvs,
):
    ny, nz = torus_of(ep)
    count, width = tok_ref.shape
    experts = router_ref.shape[1]
    total = ep * count
    groups = total // GROUP
    n_shares = width // LANES
    repeat = ep // n_shares
    dp = lax.axis_index("dp")
    me, core, y, z = place(ep, ny, nz)
    mate = (dp, at_ep(nz, y, z, 1 - core))
    z_peers = [(dp, at_ep(nz, y, lax.rem(z + k, nz), core)) for k in range(1, nz)]
    y_peers = [(dp, at_ep(nz, lax.rem(y + k, ny), z, core)) for k in range(1, ny)]
    x_peers = [(lax.rem(dp + k, n_dp), me) for k in range(1, n_dp)]
    share, twin = me // repeat, lax.rem(me, repeat)
    share_peers = [
        (dp, lax.rem(share + k, n_shares) * repeat + twin) for k in range(1, n_shares)
    ]
    enter([mate, *z_peers, *y_peers, *x_peers, *share_peers])

    def copy_of(n, ref, peer):
        return pltpu.make_async_remote_copy(
            src_ref=ref, dst_ref=ref, send_sem=sends.at[n], recv_sem=recvs.at[n],
            device_id=peer, device_id_type=MESH,
        )

    mine = y * nz + z
    for g in range(groups):
        row = jnp.dot(
            grad_ref[:, g * GROUP // count * SLOTS : (g + 1) * GROUP // count * SLOTS],
            pick_ref[g],
            preferred_element_type=f32,
        )
        table[mine, core, g : g + 1, :] = row[0:1]
    n = 0
    all_copies = []

    def part(chip, chips):
        return table.at[pl.ds(chip, chips)]

    copy = copy_of(n, table.at[mine, core], mate)
    copy.start()
    all_copies.append(copy)
    copy_of(n, table.at[mine, 1 - core], mate).wait_recv()
    n += 1
    for k, peer in enumerate(z_peers):
        copy = copy_of(n + k, part(mine, 1), peer)
        copy.start()
        all_copies.append(copy)
    for k in range(nz - 1):
        copy_of(n + k, part(y * nz + lax.rem(z - 1 - k + nz, nz), 1), mate).wait_recv()
    n += nz - 1
    for k, peer in enumerate(y_peers):
        copy = copy_of(n + k, part(y * nz, nz), peer)
        copy.start()
        all_copies.append(copy)
    for k in range(ny - 1):
        copy_of(n + k, part(lax.rem(y - 1 - k + ny, ny) * nz, nz), mate).wait_recv()
    n += ny - 1

    for g in range(groups):
        both = table[:, :, g, :]
        grad[:, g * GROUP : (g + 1) * GROUP] = both.reshape(experts, GROUP)
    inverse_token = totals[ITERS + 1 : ITERS + 2, :]
    picked_sum = totals[ITERS : ITERS + 1, :]
    member = marks_ref[...] > 0.0
    route = jnp.where(member, grad[...], 0.0)
    gates = jnp.where(member, kernels[ITERS], 0.0) / picked_sum
    grad[...] = jnp.where(
        member, (route - jnp.sum(route * gates, axis=0, keepdims=True)) / picked_sum, 0.0
    )
    for s in reversed(range(ITERS)):
        kernel = kernels[s + 1]
        row = totals[s : s + 1, :]
        column = columns[s][:, 0:1]
        slope = grad[...]
        slope = (slope - jnp.sum(slope * kernel, axis=0, keepdims=True)) / row
        moment = jnp.sum(slope * (kernel * row), axis=1, keepdims=True)
        grad[...] = (slope - moment) / column
    logit_grad = grad[...] * kernels[0]
    weighted = logit_grad * logits_ref[...]
    router = router_ref[...]
    router_wide = router.astype(f32)
    square = jnp.sum(router_wide * router_wide, axis=0, keepdims=True) + eps_norm
    square = jnp.broadcast_to(square, (LANES, experts)).T[:, 0:1]
    turn = logit_grad * (cos_scale * inverse_token) / jnp.sqrt(square)
    spread[:experts, :] = turn
    spread[experts:, :] = jnp.broadcast_to(
        jnp.sum(weighted, axis=0, keepdims=True) * inverse_token * inverse_token,
        (spread.shape[0] - experts, total),
    )

    features = slice_ref[...].reshape(total, LANES)
    product = jnp.dot(
        jnp.concatenate(split_three(turn), axis=0), features, preferred_element_type=f32
    )
    product = product[:experts] + product[experts : 2 * experts] + product[2 * experts :]
    own_router = router_ref[pl.ds(pl.multiple_of(share * LANES, LANES), LANES), :].astype(f32).T
    parts[dp] = product - own_router * (jnp.sum(weighted, axis=1, keepdims=True) / square)
    for k, peer in enumerate(x_peers):
        copy = copy_of(n + k, parts.at[dp], peer)
        copy.start()
        all_copies.append(copy)

    turned[...] = spread[:, pl.ds(pl.multiple_of(me * count // LANES * LANES, LANES), LANES)].T
    own = turned[pl.ds(pl.multiple_of(lax.rem(me, LANES // count) * count, count), count), :]
    back = jnp.zeros((count, width), f32)
    for term in split_three(own[:, :experts]):
        back += lax.dot_general(term, router, contract_last, preferred_element_type=f32)
    back_out[...] = back - tok_ref[...].astype(f32) * own[:, experts : experts + 1]

    for k in range(n_dp - 1):
        copy_of(n + k, parts.at[lax.rem(dp - 1 - k + n_dp, n_dp)], mate).wait_recv()
    n += n_dp - 1
    summed = parts[0]
    for k in range(1, n_dp):
        summed += parts[k]
    shares[share] = summed
    for k, peer in enumerate(share_peers):
        copy = copy_of(n + k, shares.at[share], peer)
        copy.start()
        all_copies.append(copy)
    for k in range(n_shares - 1):
        copy_of(n + k, shares.at[lax.rem(share - 1 - k + n_shares, n_shares)], mate).wait_recv()
    for k in range(n_shares):
        router_out[k * LANES : (k + 1) * LANES, :] = shares[k].T
    for copy in all_copies:
        copy.wait_send()


def router_backward(gate_grad, pick, saved, features, tokens, router, ep, n_dp):
    ny, nz = torus_of(ep)
    kernels, columns, totals, logits, marks = saved
    count, width = tokens.shape
    experts = router.shape[1]
    total = ep * count
    n_shares = width // LANES
    copies = 1 + nz - 1 + ny - 1 + n_dp - 1 + n_shares - 1
    vmem = pl.BlockSpec(memory_space=pltpu.VMEM)
    return pl.pallas_call(
        functools.partial(router_kernel, ep, n_dp),
        out_shape=(
            jax.ShapeDtypeStruct((count, width), f32),
            jax.ShapeDtypeStruct((width, experts), f32),
        ),
        in_specs=[vmem] * 10,
        out_specs=(vmem, vmem),
        scratch_shapes=[
            pltpu.VMEM((ny * nz, 2, total // GROUP, GROUP), f32),
            pltpu.VMEM((experts, total), f32),
            pltpu.VMEM((LANES, total), f32),
            pltpu.VMEM((LANES, LANES), f32),
            pltpu.VMEM((n_dp, experts, LANES), f32),
            pltpu.VMEM((n_shares, experts, LANES), f32),
            pltpu.SemaphoreType.DMA((copies,)),
            pltpu.SemaphoreType.DMA((copies,)),
        ],
        compiler_params=pltpu.CompilerParams(
            collective_id=2, has_side_effects=True, vmem_limit_bytes=40 * 2**20
        ),
    )(
        jnp.broadcast_to(gate_grad[None, :], (8, gate_grad.shape[0])),
        pick,
        kernels,
        columns,
        totals,
        logits,
        marks,
        features,
        tokens,
        router,
    )


def per_device(ep, n_dp, tokens, cotangent, assign, w_router, w_gate, w_up, w_down):
    local_tokens = tokens[0]
    count, width = local_tokens.shape
    experts = w_router.shape[1]
    rows, cotangent_rows, rows_gate, pick, kernels, columns, totals, logits, marks, features = dispatch(
        local_tokens, cotangent[0], assign[0], w_router, ep
    )
    gate_matrix, up_matrix, down_matrix = w_gate[0], w_up[0], w_down[0]

    def reduced(left, right):
        product = lax.dot_general(left, right, contract_first, preferred_element_type=f32)
        return lax.psum_scatter(
            product.astype(bf16), "dp", scatter_dimension=0, tiled=True
        )[None]

    gate_linear = jnp.dot(rows, gate_matrix, preferred_element_type=f32)
    up_linear = jnp.dot(rows, up_matrix, preferred_element_type=f32)
    sigmoid_gate = jax.nn.sigmoid(gate_linear)
    activation = gate_linear * sigmoid_gate
    product = activation * up_linear
    hidden = product.astype(bf16)
    weighted = (rows_gate * product).astype(bf16)
    grad_down = reduced(cotangent_rows, weighted)
    raw_back = jnp.dot(cotangent_rows, down_matrix, preferred_element_type=f32)
    gate_grad = jnp.sum(raw_back * hidden.astype(f32), axis=1).astype(bf16)
    scaled_back = rows_gate * raw_back
    up_delta = (scaled_back * activation).astype(bf16)
    gate_delta = (
        scaled_back * up_linear * sigmoid_gate * (1.0 + gate_linear * (1.0 - sigmoid_gate))
    ).astype(bf16)
    grad_up = reduced(rows, up_delta)
    grad_gate = reduced(rows, gate_delta)
    route_back = (
        lax.dot_general(gate_delta, gate_matrix, contract_last, preferred_element_type=f32)
        + lax.dot_general(up_delta, up_matrix, contract_last, preferred_element_type=f32)
    ).astype(bf16)
    back_rows = lax.all_to_all(
        route_back.reshape(ep, SLOTS, width), "ep", split_axis=0, concat_axis=0, tiled=True
    )
    router_back, grad_router = router_backward(
        gate_grad, pick, (kernels, columns, totals, logits, marks), features, local_tokens, w_router, ep, n_dp
    )

    named = jnp.any(
        assign[0][:, :, None] == jnp.arange(experts, dtype=jnp.int32), axis=1
    ).astype(bf16)
    order = jnp.arange(count)
    earlier = (order[:, None] > order[None, :]).astype(bf16)
    rank = jnp.dot(earlier, named, preferred_element_type=f32)
    slot_of = jnp.where(named > 0, rank, -1.0)
    token_slots = (
        slot_of[:, :, None] == jnp.arange(SLOTS, dtype=f32)
    ).astype(bf16).reshape(count, experts * SLOTS)
    expert_back = jnp.dot(token_slots, back_rows.reshape(-1, width), preferred_element_type=f32)
    grad_tokens = (expert_back + router_back).astype(bf16)[None]
    return grad_tokens, grad_router, grad_gate, grad_up, grad_down


def solution(mesh):
    return jax.shard_map(
        functools.partial(per_device, mesh.shape["ep"], mesh.shape["dp"]),
        mesh=mesh,
        in_specs=(
            P("dp", "ep", None),
            P("dp", "ep", None),
            P("dp", "ep", None),
            P(),
            P("ep", None, None),
            P("ep", None, None),
            P("ep", None, None),
        ),
        out_specs=(
            P("dp", "ep", None),
            P(),
            P("ep", "dp", None),
            P("ep", "dp", None),
            P("ep", "dp", None),
        ),
        check_vma=False,
    )
```

time: 1250 us -> 245 us (0.20)
  blocking collectives: 786 us -> 0 us
  waiting for transfers between devices: 328 us -> 11.1 us
  Pallas kernels: 0 us -> 151 us
  starting transfers between devices: 30.5 us -> 6.02 us
  other arithmetic: 24.4 us -> 1.22 us
    psum x6 -> x0, blocking collectives: 786 us -> none  [the longest x3 405 us: per_device(): moment = lax.psum(jnp.sum(scaled_grad * scaled, axis=0), 'ep')]
    psum x1 -> x0, waiting for transfers between devices: 230 us -> none  [per_device(): grad_router = lax.psum(router_part, ('dp', 'ep'))]
    pallas_call x0 -> x2, Pallas kernels: none -> 151 us  [the longest x1 78.5 us: dispatch(): pl.pallas_call(functools.partial(dispatch_kernel, ep), out_shape=(shape((...]
    all_to_all x5 -> x1, waiting for transfers between devices: 98.5 us -> 0.01 us  [per_device(): lax.all_to_all(route_back.reshape(ep, SLOTS, width), 'ep', split_axis=0,...]
    all_to_all x5 -> x1, starting transfers between devices: 30.2 us -> 5.72 us  [per_device(): lax.all_to_all(route_back.reshape(ep, SLOTS, width), 'ep', split_axis=0,...]
    reduce_sum x19 -> x0, other arithmetic: 14.1 us -> none  [the longest x3 4.61 us: per_device(): moment = lax.psum(jnp.sum(scaled_grad * scaled, axis=0), 'ep')]
    dot_general x16 -> x10, matrix products: 45.9 us -> 42.5 us  [the longest x3 15.3 us: reduced(): lax.dot_general(left, right, contract_first, preferred_element_type=f32)]
  transfers between devices with their start and end apart: 7 -> 4, of which waited for: 5 -> 1; matrix products, arithmetic and copies ran while one was open for 4% -> 11% of each run, Pallas kernels for 0% -> 30%
where the time goes in v1:
time: 245 us
  Pallas kernels  151 us (62%)
  matrix products  42.5 us (17%)
  local copies, waits for them, and re-layouts  18.9 us (8%)
  between operations  14 us (6%)
  waiting for transfers between devices  11.1 us (5%)
  starting transfers between devices  6.02 us (2%)
    pallas_call x1, Pallas kernels, dispatch(): pl.pallas_call(functools.partial(dispatch_kernel, ep), out_shape=(shape((...  78.5 us
    pallas_call x1, Pallas kernels, router_backward(): pl.pallas_call(functools.partial(router_kernel, ep, n_dp), out_shape=(jax...  72.3 us
    unnamed x57, local copies, waits for them, and re-layouts  18.3 us
    dot_general x3, matrix products, reduced(): lax.dot_general(left, right, contract_first, preferred_element_type=f32)  15.3 us
    reduce_scatter x3, waiting for transfers between devices, reduced(): lax.psum_scatter(product.astype(bf16), 'dp', scatter_dimension=0, tiled=T...  11 us
    dot_general x1, matrix products, per_device(): gate_linear = jnp.dot(rows, gate_matrix, preferred_element_type=f32)  7.03 us
    dot_general x1, matrix products, per_device(): up_linear = jnp.dot(rows, up_matrix, preferred_element_type=f32)  6.26 us
    all_to_all x1, starting transfers between devices, per_device(): lax.all_to_all(route_back.reshape(ep, SLOTS, width), 'ep', split_axis=0,...  5.72 us
  transfers between devices with their start and end apart: 4, of which 1 were waited for; matrix products, arithmetic and copies ran while one was open for 11% of the time, Pallas kernels for 30%

profile of v1, /device:TPU:1, one launch (start us, length us, event | category | flops | bytes accessed | tf_op | source)
XLA Modules:
  0.0 244.5 jit_solution(13996781979781094013)
XLA Ops:
  8.1 2.0 copy.28.router_ref
  10.1 1.0 copy-done.1
  12.9 78.5 %shard_map.110 = (bf16[512,2048]{1,0:T(8,128)(2,1)S(1)}, bf16[512,2048]{1,0:T(8,128)(2,1)}, f32[512,1]{1,0:T(8,128)S(1)}, bf16[8,64,256]{2,1,0:T(8,128)(2,1)S(1)...) custom-call(bf16[32,2048]{1,0:T(8,128)(2,1)S(1)} %bitcast.48, ...), custom_call_target="tpu_custom_call" | custom-call | tf_op jit(solution)/shard_map/pallas_call | solution.py:304
  91.5 6.3 %fusion.6 = f32[512,768]{1,0:T(8,128)} fusion(bf16[512,2048]{1,0:T(8,128)(2,1)S(1)} %get-tuple-element.19, bf16[1,2048,768]{2,1,0:T(8,128)(2,1)} %param.12), kind=kOutput, calls=%fused_computation.10 | convolution fusion | flops 1610612736 | bytes 6815744 | tf_op jit(solution)/shard_map/dot_general | solution.py:557
  97.8 3.0 %fusion.8 = f32[512,768]{1,0:T(8,128)} fusion(bf16[512,2048]{1,0:T(8,128)(2,1)S(1)} %copy-done.24, bf16[1,2048,768]{2,1,0:T(8,128)(2,1)S(1)} %copy-done.22), kind=kOutput, calls=%fused_computation.12 | convolution fusion | flops 1610612736 | bytes 6815744 | tf_op jit(solution)/shard_map/dot_general | solution.py:564
  100.8 1.1 reduce
  101.9 7.0 %multiply_convert_fusion.2 = (bf16[512,768]{1,0:T(8,128)(2,1)S(1)}, bf16[512]{0:T(512)(128)(2,1)}, bf16[512,768]{1,0:T(8,128)(2,1)}, f32[512,768]{1,0:T(8,128)}) fusion(f32[512,768]{1,0:T(8,128)} %fusion.6, f32[512,768]{1,0:T(8,128)} %fusion.8, f32[512]{0:T(512)S(1)} %reduce, bf16[512,2048]{1,0:T(8,128)(2,1)} %copy-done.19, ...), kind=kOutput, calls=%fused_computation.23 | convolution fusion | flops 1618083328 | bytes 11537408 | tf_op jit(solution)/shard_map/dot_general | solution.py:556
  108.9 0.9 copy-done.26
  109.9 3.5 %convolution_convert_fusion.2 = bf16[2048,768]{1,0:T(8,128)(2,1)} fusion(bf16[512,2048]{1,0:T(8,128)(2,1)S(1)} %copy-done.20, bf16[512,768]{1,0:T(8,128)(2,1)S(1)} %get-tuple-element.49), kind=kOutput, calls=%fused_computation.3 | convolution fusion | flops 1612185600 | bytes 6029312 | tf_op jit(solution)/shard_map/dot_general | solution.py:551
  113.6 5.3 %convolution_convert_fusion.1 = bf16[2048,768]{1,0:T(8,128)(2,1)} fusion(bf16[512,2048]{1,0:T(8,128)(2,1)} %copy-done.19, bf16[512,768]{1,0:T(8,128)(2,1)} %get-tuple-element.51), kind=kOutput, calls=%fused_computation.2 | convolution fusion | flops 1612185600 | bytes 6029312 | tf_op jit(solution)/shard_map/dot_general | solution.py:551
  119.0 6.5 %convolution_convert_fusion = bf16[2048,768]{1,0:T(8,128)(2,1)} fusion(bf16[512,2048]{1,0:T(8,128)(2,1)} %get-tuple-element.18, f32[512]{0:T(512)S(1)} %reduce, f32[512,768]{1,0:T(8,128)} %fusion.6, f32[512,768]{1,0:T(8,128)} %get-tuple-element.52), kind=kOutput, calls=%fused_computation.1 | convolution fusion | flops 1614938112 | bytes 8390656 | tf_op jit(solution)/shard_map/dot_general | solution.py:551
  125.5 3.1 %fusion = f32[512,2048]{1,0:T(8,128)S(1)} fusion(bf16[512,768]{1,0:T(8,128)(2,1)} %copy-done.26, bf16[1,2048,768]{2,1,0:T(8,128)(2,1)S(1)} %copy-done), kind=kOutput, calls=%fused_computation.4 | convolution fusion | flops 1610612736 | bytes 8126464 | tf_op jit(solution)/shard_map/dot_general | solution.py:574
  128.6 3.2 %fusion.12 = bf16[64,8,2048]{2,1,0:T(8,128)(2,1)} fusion(f32[512,2048]{1,0:T(8,128)S(1)} %fusion, bf16[512,768]{1,0:T(8,128)(2,1)S(1)} %copy-done.25, bf16[1,2048,768]{2,1,0:T(8,128)(2,1)S(1)} %copy-done.23), kind=kOutput, calls=%fused_computation.14 | convolution fusion | flops 1612709888 | bytes 10223616 | tf_op jit(solution)/shard_map/dot_general | solution.py:575
  131.8 5.7 %all-to-all-start = ((bf16[64,8,2048]{2,1,0:T(8,128)(2,1)}), bf16[64,8,2048]{2,1,0:T(8,128)(2,1)}, u32[]{:S(2)}, u32[]{:S(2)}) async-start(bf16[64,8,2048]{2,1,0:T(8,128)(2,1)} %fusion.12), calls=%async_computation | async-start | bytes 4194304 | tf_op jit(solution)/shard_map/all_to_all | solution.py:577
  138.2 1.0 copy-done.2
  139.2 1.6 copy-done.3
  140.9 1.0 copy-done.6
  141.9 1.0 copy-done.8
  143.0 1.0 copy-done.10
  145.7 72.3 %shard_map.111 = (f32[32,2048]{1,0:T(8,128)S(1)}, f32[2048,64]{1,0:T(8,128)S(1)}) custom-call(bf16[8,512]{1,0:T(8,128)(2,1)S(1)} %broadcast_in_dim.28.grad_ref, bf16[8,64,256]{2,1,0:T(8,128)(2,1)S(1)} %get-tuple-element.20.pick_ref, f32[4,64,2048]{2,1,0:T(8,128)S(1)} %copy-done.3, f32[3,64,128]{2,1,0:T(8,128)S(1)} %copy-done.16, f32[8,2048]{1,0:T(8,128)S(1)} %copy-done.18, ...), custom_call_target="tpu_custom_call" | custom-call | tf_op jit(solution)/shard_map/pallas_call | solution.py:506
  218.0 1.0 copy-done.4
  219.7 2.3 copy.31
  222.3 4.6 %fusion.17 = bf16[1,32,2048]{2,1,0:T(8,128)(2,1)} fusion(f32[32,2048]{1,0:T(8,128)} %copy-done.21, bf16[64,8,2048]{2,1,0:T(8,128)(2,1)} %all-to-all-done, f32[32,64]{1,0:T(8,128)S(1)} %convolution_select_fusion), kind=kOutput, calls=%fused_computation.18 | convolution fusion | flops 67256320 | bytes 2498560 | tf_op jit(solution)/shard_map/dot_general | solution.py:594
  227.0 11.0 %reduce-scatter.8.cloned.1.call-done = bf16[512,768]{1,0:T(8,128)(2,1)} async-done(((bf16[2048,768]{1,0:T(8,128)(2,1)}), bf16[512,768]{1,0:T(8,128)(2,1)}) %reduce-scatter.8.cloned.1.call-update) | async-done | bytes 786448 | tf_op jit(solution)/shard_map/reduce_scatter | solution.py:552
  (59 shorter events, 6.5 us)
Async XLA Ops:
  7.2 94.7 %copy-start = (bf16[1,2048,768]{2,1,0:T(8,128)(2,1)S(1)}, bf16[1,2048,768]{2,1,0:T(8,128)(2,1)}, u32[]{:S(2)}) copy-start(bf16[1,2048,768]{2,1,0:T(8,128)(2,1)} %param.11) | copy-start | bytes 9437188
  7.2 219.8 %reduce-scatter.4.cloned.1.call-start = ((), (), s32[]{:S(2)}) async-start(), calls=%async_computation.4 | async-start | bytes 3932160 | tf_op jit(solution)/shard_map/reduce_scatter | solution.py:552
  10.1 1.0 copy-start.1
  91.4 6.4 %copy-start.5 = (f32[64,2048]{1,0:T(8,128)}, f32[64,2048]{1,0:T(8,128)S(1)}, u32[]{:S(2)}) copy-start(f32[64,2048]{1,0:T(8,128)S(1)} %get-tuple-element.24.logits_ref) | copy-start | bytes 1572868
  91.4 6.4 %copy-start.7 = (f32[64,2048]{1,0:T(8,128)}, f32[64,2048]{1,0:T(8,128)S(1)}, u32[]{:S(2)}) copy-start(f32[64,2048]{1,0:T(8,128)S(1)} %get-tuple-element.25.marks_ref) | copy-start | bytes 1572868
  91.4 6.3 %copy-start.9 = (bf16[64,32,128]{2,1,0:T(8,128)(2,1)}, bf16[64,32,128]{2,1,0:T(8,128)(2,1)S(1)}, u32[]{:S(2)}) copy-start(bf16[64,32,128]{2,1,0:T(8,128)(2,1)S(1)} %get-tuple-element.26.slice_ref) | copy-start | bytes 1572868
  91.4 6.3 %copy-start.13 = (f32[512,1]{1,0:T(8,128)}, f32[512,1]{1,0:T(8,128)S(1)}, u32[]{:S(2)}) copy-start(f32[512,1]{1,0:T(8,128)S(1)} %get-tuple-element.17) | copy-start | bytes 6148
  91.5 6.3 %copy-start.15 = (f32[3,64,128]{2,1,0:T(8,128)}, f32[3,64,128]{2,1,0:T(8,128)S(1)}, u32[]{:S(2)}) copy-start(f32[3,64,128]{2,1,0:T(8,128)S(1)} %get-tuple-element.22.columns) | copy-start | bytes 294916
  91.5 6.3 %copy-start.17 = (f32[8,2048]{1,0:T(8,128)}, f32[8,2048]{1,0:T(8,128)S(1)}, u32[]{:S(2)}) copy-start(f32[8,2048]{1,0:T(8,128)S(1)} %get-tuple-element.23.totals) | copy-start | bytes 196612
  91.5 6.3 %copy-start.19 = (bf16[512,2048]{1,0:T(8,128)(2,1)}, bf16[512,2048]{1,0:T(8,128)(2,1)S(1)}, u32[]{:S(2)}) copy-start(bf16[512,2048]{1,0:T(8,128)(2,1)S(1)} %get-tuple-element.19) | copy-start | bytes 6291460
  91.5 6.3 %copy-start.22 = (bf16[1,2048,768]{2,1,0:T(8,128)(2,1)S(1)}, bf16[1,2048,768]{2,1,0:T(8,128)(2,1)}, u32[]{:S(2)}) copy-start(bf16[1,2048,768]{2,1,0:T(8,128)(2,1)} %param.13) | copy-start | bytes 9437188
  91.5 6.3 %copy-start.24 = (bf16[512,2048]{1,0:T(8,128)(2,1)S(1)}, bf16[512,2048]{1,0:T(8,128)(2,1)}, u32[]{:S(2)}) copy-start(bf16[512,2048]{1,0:T(8,128)(2,1)} %get-tuple-element.18) | copy-start | bytes 6291460
  101.9 8.0 %copy-start.20 = (bf16[512,2048]{1,0:T(8,128)(2,1)S(1)}, bf16[512,2048]{1,0:T(8,128)(2,1)}, u32[]{:S(2)}) copy-start(bf16[512,2048]{1,0:T(8,128)(2,1)} %copy-done.19) | copy-start | bytes 6291460
  113.4 113.6 %reduce-scatter.6.cloned.1.call-start = ((), (), s32[]{:S(2)}) async-start(), calls=%async_computation.5 | async-start | bytes 3932160 | tf_op jit(solution)/shard_map/reduce_scatter | solution.py:552
  118.9 119.1 %reduce-scatter.8.cloned.1.call-start = ((), (), s32[]{:S(2)}) async-start(), calls=%async_computation.6 | async-start | bytes 3932160 | tf_op jit(solution)/shard_map/reduce_scatter | solution.py:552
  125.5 3.1 %copy-start.23 = (bf16[1,2048,768]{2,1,0:T(8,128)(2,1)S(1)}, bf16[1,2048,768]{2,1,0:T(8,128)(2,1)}, u32[]{:S(2)}) copy-start(bf16[1,2048,768]{2,1,0:T(8,128)(2,1)} %param.12) | copy-start | bytes 9437188
  125.5 3.1 %copy-start.25 = (bf16[512,768]{1,0:T(8,128)(2,1)S(1)}, bf16[512,768]{1,0:T(8,128)(2,1)}, u32[]{:S(2)}) copy-start(bf16[512,768]{1,0:T(8,128)(2,1)} %get-tuple-element.51) | copy-start | bytes 2359300
  131.8 6.4 %copy-start.12 = (bf16[1,32,2048]{2,1,0:T(8,128)(2,1)S(1)}, bf16[1,32,2048]{2,1,0:T(8,128)(2,1)}, u32[]{:S(2)}) copy-start(bf16[1,32,2048]{2,1,0:T(8,128)(2,1)} %param.7) | copy-start | bytes 393220
  131.8 90.5 %all-to-all-start = ((bf16[64,8,2048]{2,1,0:T(8,128)(2,1)}), bf16[64,8,2048]{2,1,0:T(8,128)(2,1)}, u32[]{:S(2)}, u32[]{:S(2)}) async-start(bf16[64,8,2048]{2,1,0:T(8,128)(2,1)} %fusion.12), calls=%async_computation | async-start | bytes 4194304 | tf_op jit(solution)/shard_map/all_to_all | solution.py:577
  138.2 1.0 copy-start.2
  139.2 1.6 copy-start.3
  140.9 1.0 copy-start.6
  141.9 1.0 copy-start.8
  142.9 1.0 copy-start.10
  (7 other events, 6.2 us)
Sparse Core Ops, SparseCore 0:
  113.5 37.0 reduce-scatter.3
  153.7 40.5 reduce-scatter.5
  197.4 40.5 reduce-scatter.7

commit v2 on v1

--- a/solution.py
+++ b/solution.py
@@ -23,7 +23,7 @@
 
 
 def torus_of(ep):
-    ny = 4
+    ny = max(1, min(4, ep // 4))
     return ny, ep // (2 * ny)
 
 
@@ -43,6 +43,8 @@
                     out.append((axis, sign, piece))
 
         def onward(at, n):
+            if n == 1:
+                return ()
             if at == 0:
                 return (1, -1)
             return ((1,) if at > 0 else (-1,)) if abs(at) < n // 2 else ()
@@ -341,7 +343,7 @@
     return high, middle, (rest - middle.astype(f32)).astype(bf16)
 
 
-def router_kernel(
+def backward_kernel(
     ep,
     n_dp,
     grad_ref,
@@ -354,16 +356,43 @@
     slice_ref,
     tok_ref,
     router_ref,
-    back_out,
+    rows_ref,
+    cot_rows_ref,
+    gate_delta,
+    up_delta,
+    weighted_ref,
+    slots_ref,
+    w_gate_hbm,
+    w_up_hbm,
+    tokens_out,
     router_out,
+    gate_out,
+    up_out,
+    down_out,
+    w_gate,
+    w_up,
     table,
     grad,
     spread,
     turned,
     parts,
     shares,
+    route_back,
+    back_rows,
+    sent_far,
+    got_far,
+    sent_near,
+    got_near,
+    own_sum,
     sends,
     recvs,
+    row_sends,
+    row_recvs,
+    far_sends,
+    far_recvs,
+    near_sends,
+    near_recvs,
+    weight_sems,
 ):
     ny, nz = torus_of(ep)
     count, width = tok_ref.shape
@@ -372,22 +401,74 @@
     groups = total // GROUP
     n_shares = width // LANES
     repeat = ep // n_shares
+    chunk = width // n_dp // 2
     dp = lax.axis_index("dp")
     me, core, y, z = place(ep, ny, nz)
     mate = (dp, at_ep(nz, y, z, 1 - core))
     z_peers = [(dp, at_ep(nz, y, lax.rem(z + k, nz), core)) for k in range(1, nz)]
     y_peers = [(dp, at_ep(nz, lax.rem(y + k, ny), z, core)) for k in range(1, ny)]
     x_peers = [(lax.rem(dp + k, n_dp), me) for k in range(1, n_dp)]
+    right, left = (lax.rem(dp + 1, n_dp), me), (lax.rem(dp + n_dp - 1, n_dp), me)
     share, twin = me // repeat, lax.rem(me, repeat)
     share_peers = [
         (dp, lax.rem(share + k, n_shares) * repeat + twin) for k in range(1, n_shares)
     ]
-    enter([mate, *z_peers, *y_peers, *x_peers, *share_peers])
+
+    fetch_gate = pltpu.make_async_copy(w_gate_hbm, w_gate, weight_sems.at[0])
+    fetch_up = pltpu.make_async_copy(w_up_hbm, w_up, weight_sems.at[1])
+    fetch_gate.start()
+    fetch_up.start()
+
+    barrier = pltpu.get_barrier_semaphore()
+
+    def greet(k, carry):
+        pl.semaphore_signal(
+            barrier, inc=1, device_id=(dp, lax.rem(me + k, ep)), device_id_type=MESH
+        )
+        return carry
+
+    lax.fori_loop(1, ep, greet, 0)
+    for peer in x_peers:
+        pl.semaphore_signal(barrier, inc=1, device_id=peer, device_id_type=MESH)
+    pl.semaphore_wait(barrier, ep - 1 + n_dp - 1)
+
+    started = []
 
     def copy_of(n, ref, peer):
         return pltpu.make_async_remote_copy(
             src_ref=ref, dst_ref=ref, send_sem=sends.at[n], recv_sem=recvs.at[n],
             device_id=peer, device_id_type=MESH,
+        )
+
+    def start(copy):
+        copy.start()
+        started.append(copy)
+
+    def far_copy(a, side):
+        return pltpu.make_async_remote_copy(
+            src_ref=sent_far.at[a, side], dst_ref=got_far.at[a, side],
+            send_sem=far_sends.at[a, side], recv_sem=far_recvs.at[a, side],
+            device_id=(right, left)[side], device_id_type=MESH,
+        )
+
+    def near_copy(a, side, half):
+        return pltpu.make_async_remote_copy(
+            src_ref=sent_near.at[a, side, half], dst_ref=got_near.at[a, side, half],
+            send_sem=near_sends.at[a, side, half], recv_sem=near_recvs.at[a, side, half],
+            device_id=(right, left)[side], device_id_type=MESH,
+        )
+
+    pairs = ((cot_rows_ref, weighted_ref), (rows_ref, up_delta), (rows_ref, gate_delta))
+    outs = (down_out, up_out, gate_out)
+    arrays = range(3)
+
+    def gradient(a, away, half):
+        block = lax.rem(dp + away, n_dp)
+        first = pl.multiple_of(block * (2 * chunk) + half * chunk, chunk)
+        left_rows, right_rows = pairs[a]
+        return lax.dot_general(
+            left_rows[:, pl.ds(first, chunk)], right_rows[...], contract_first,
+            preferred_element_type=f32,
         )
 
     mine = y * nz + z
@@ -399,27 +480,77 @@
         )
         table[mine, core, g : g + 1, :] = row[0:1]
     n = 0
-    all_copies = []
 
     def part(chip, chips):
         return table.at[pl.ds(chip, chips)]
 
-    copy = copy_of(n, table.at[mine, core], mate)
-    copy.start()
-    all_copies.append(copy)
+    start(copy_of(n, table.at[mine, core], mate))
+
+    def far(a):
+        for side in range(2):
+            sent_far[a, side] = gradient(a, 2, side).astype(bf16)
+            start(far_copy(a, side))
+
+    def near_plain(a):
+        for side in range(2):
+            sent_near[a, side, 1 - side] = gradient(a, (1, n_dp - 1)[side], 1 - side).astype(bf16)
+            start(near_copy(a, side, 1 - side))
+
+    def near_joined(a):
+        for side in range(2):
+            mixed = gradient(a, (1, n_dp - 1)[side], side)
+            far_copy(a, side).wait_recv()
+            sent_near[a, side, side] = (mixed + got_far[a, side].astype(f32)).astype(bf16)
+            start(near_copy(a, side, side))
+
+    ring = n_dp == 4
+    if ring:
+        far(0)
     copy_of(n, table.at[mine, 1 - core], mate).wait_recv()
     n += 1
     for k, peer in enumerate(z_peers):
-        copy = copy_of(n + k, part(mine, 1), peer)
-        copy.start()
-        all_copies.append(copy)
+        start(copy_of(n + k, part(mine, 1), peer))
+    if ring:
+        far(1)
+        far(2)
     for k in range(nz - 1):
         copy_of(n + k, part(y * nz + lax.rem(z - 1 - k + nz, nz), 1), mate).wait_recv()
     n += nz - 1
     for k, peer in enumerate(y_peers):
-        copy = copy_of(n + k, part(y * nz, nz), peer)
-        copy.start()
-        all_copies.append(copy)
+        start(copy_of(n + k, part(y * nz, nz), peer))
+
+    fetch_gate.wait()
+    fetch_up.wait()
+    pieces = 4
+    rows_each = ep // pieces
+
+    def rows_back(q, carry):
+        rows = pl.ds(pl.multiple_of(q * rows_each * SLOTS, rows_each * SLOTS), rows_each * SLOTS)
+        value = lax.dot_general(
+            gate_delta[rows, :], w_gate[...], contract_last, preferred_element_type=f32
+        ) + lax.dot_general(up_delta[rows, :], w_up[...], contract_last, preferred_element_type=f32)
+        route_back[pl.ds(q * rows_each, rows_each)] = value.astype(bf16).reshape(
+            rows_each, SLOTS, width
+        )
+        return carry
+
+    lax.fori_loop(0, pieces, rows_back, 0)
+
+    def row_copy(k, from_block, to_block, peer):
+        return pltpu.make_async_remote_copy(
+            src_ref=route_back.at[from_block], dst_ref=back_rows.at[to_block],
+            send_sem=row_sends.at[k], recv_sem=row_recvs.at[k],
+            device_id=(dp, peer), device_id_type=MESH,
+        )
+
+    def send_rows(k, carry):
+        peer = lax.rem(me + k, ep)
+        row_copy(k, peer, me, peer).start()
+        return carry
+
+    lax.fori_loop(1, ep, send_rows, 0)
+    back_rows[me] = route_back[me]
+
     for k in range(ny - 1):
         copy_of(n + k, part(lax.rem(y - 1 - k + ny, ny) * nz, nz), mate).wait_recv()
     n += ny - 1
@@ -464,16 +595,24 @@
     own_router = router_ref[pl.ds(pl.multiple_of(share * LANES, LANES), LANES), :].astype(f32).T
     parts[dp] = product - own_router * (jnp.sum(weighted, axis=1, keepdims=True) / square)
     for k, peer in enumerate(x_peers):
-        copy = copy_of(n + k, parts.at[dp], peer)
-        copy.start()
-        all_copies.append(copy)
+        start(copy_of(n + k, parts.at[dp], peer))
+
+    if ring:
+        for a in arrays:
+            near_plain(a)
+        for a in arrays:
+            near_joined(a)
 
     turned[...] = spread[:, pl.ds(pl.multiple_of(me * count // LANES * LANES, LANES), LANES)].T
     own = turned[pl.ds(pl.multiple_of(lax.rem(me, LANES // count) * count, count), count), :]
     back = jnp.zeros((count, width), f32)
     for term in split_three(own[:, :experts]):
         back += lax.dot_general(term, router, contract_last, preferred_element_type=f32)
-    back_out[...] = back - tok_ref[...].astype(f32) * own[:, experts : experts + 1]
+    back -= tok_ref[...].astype(f32) * own[:, experts : experts + 1]
+
+    for a in arrays:
+        for half in range(2):
+            own_sum[a, half] = gradient(a, 0, half)
 
     for k in range(n_dp - 1):
         copy_of(n + k, parts.at[lax.rem(dp - 1 - k + n_dp, n_dp)], mate).wait_recv()
@@ -483,46 +622,103 @@
         summed += parts[k]
     shares[share] = summed
     for k, peer in enumerate(share_peers):
-        copy = copy_of(n + k, shares.at[share], peer)
-        copy.start()
-        all_copies.append(copy)
+        start(copy_of(n + k, shares.at[share], peer))
+
+    def got_rows(k, carry):
+        block = lax.rem(me - k + ep, ep)
+        row_copy(k, block, block, block).wait_recv()
+        return carry
+
+    lax.fori_loop(1, ep, got_rows, 0)
+    tokens_out[...] = (
+        back
+        + jnp.dot(
+            slots_ref[...], back_rows[...].reshape(ep * SLOTS, width), preferred_element_type=f32
+        )
+    ).astype(bf16)
+
     for k in range(n_shares - 1):
         copy_of(n + k, shares.at[lax.rem(share - 1 - k + n_shares, n_shares)], mate).wait_recv()
     for k in range(n_shares):
         router_out[k * LANES : (k + 1) * LANES, :] = shares[k].T
-    for copy in all_copies:
+
+    def finish(a, half):
+        value = own_sum[a, half]
+        if ring:
+            for side in range(2):
+                near_copy(a, side, half).wait_recv()
+                value += got_near[a, side, half].astype(f32)
+        outs[a][half * chunk : (half + 1) * chunk, :] = value.astype(bf16)
+
+    for a in arrays:
+        for half in range(2):
+            finish(a, half)
+
+    def sent_rows(k, carry):
+        peer = lax.rem(me + k, ep)
+        row_copy(k, peer, me, peer).wait_send()
+        return carry
+
+    lax.fori_loop(1, ep, sent_rows, 0)
+    for copy in started:
         copy.wait_send()
 
 
-def router_backward(gate_grad, pick, saved, features, tokens, router, ep, n_dp):
+def backward(
+    gate_grad, pick, saved, features, tokens, router, rows, cotangent_rows, deltas, slots, weights, ep, n_dp
+):
     ny, nz = torus_of(ep)
     kernels, columns, totals, logits, marks = saved
     count, width = tokens.shape
     experts = router.shape[1]
+    hidden_units = deltas[0].shape[1]
     total = ep * count
     n_shares = width // LANES
     copies = 1 + nz - 1 + ny - 1 + n_dp - 1 + n_shares - 1
+    chunk = width // n_dp // 2
     vmem = pl.BlockSpec(memory_space=pltpu.VMEM)
+    anywhere = pl.BlockSpec(memory_space=pl.ANY)
+    dma = pltpu.SemaphoreType.DMA
+    gradient = jax.ShapeDtypeStruct((2 * chunk, hidden_units), bf16)
     return pl.pallas_call(
-        functools.partial(router_kernel, ep, n_dp),
+        functools.partial(backward_kernel, ep, n_dp),
         out_shape=(
-            jax.ShapeDtypeStruct((count, width), f32),
+            jax.ShapeDtypeStruct((count, width), bf16),
             jax.ShapeDtypeStruct((width, experts), f32),
+            gradient,
+            gradient,
+            gradient,
         ),
-        in_specs=[vmem] * 10,
-        out_specs=(vmem, vmem),
+        in_specs=[vmem] * 16 + [anywhere] * 2,
+        out_specs=(vmem,) * 5,
         scratch_shapes=[
+            pltpu.VMEM((width, hidden_units), bf16),
+            pltpu.VMEM((width, hidden_units), bf16),
             pltpu.VMEM((ny * nz, 2, total // GROUP, GROUP), f32),
             pltpu.VMEM((experts, total), f32),
             pltpu.VMEM((LANES, total), f32),
             pltpu.VMEM((LANES, LANES), f32),
             pltpu.VMEM((n_dp, experts, LANES), f32),
             pltpu.VMEM((n_shares, experts, LANES), f32),
-            pltpu.SemaphoreType.DMA((copies,)),
-            pltpu.SemaphoreType.DMA((copies,)),
+            pltpu.VMEM((ep, SLOTS, width), bf16),
+            pltpu.VMEM((ep, SLOTS, width), bf16),
+            pltpu.VMEM((3, 2, chunk, hidden_units), bf16),
+            pltpu.VMEM((3, 2, chunk, hidden_units), bf16),
+            pltpu.VMEM((3, 2, 2, chunk, hidden_units), bf16),
+            pltpu.VMEM((3, 2, 2, chunk, hidden_units), bf16),
+            pltpu.VMEM((3, 2, chunk, hidden_units), f32),
+            dma((copies,)),
+            dma((copies,)),
+            dma((ep,)),
+            dma((ep,)),
+            dma((3, 2)),
+            dma((3, 2)),
+            dma((3, 2, 2)),
+            dma((3, 2, 2)),
+            dma((2,)),
         ],
         compiler_params=pltpu.CompilerParams(
-            collective_id=2, has_side_effects=True, vmem_limit_bytes=40 * 2**20
+            collective_id=2, has_side_effects=True, vmem_limit_bytes=58 * 2**20
         ),
     )(
         jnp.broadcast_to(gate_grad[None, :], (8, gate_grad.shape[0])),
@@ -535,6 +731,11 @@
         features,
         tokens,
         router,
+        rows,
+        cotangent_rows,
+        *deltas,
+        slots,
+        *weights,
     )
 
 
@@ -547,40 +748,6 @@
     )
     gate_matrix, up_matrix, down_matrix = w_gate[0], w_up[0], w_down[0]
 
-    def reduced(left, right):
-        product = lax.dot_general(left, right, contract_first, preferred_element_type=f32)
-        return lax.psum_scatter(
-            product.astype(bf16), "dp", scatter_dimension=0, tiled=True
-        )[None]
-
-    gate_linear = jnp.dot(rows, gate_matrix, preferred_element_type=f32)
-    up_linear = jnp.dot(rows, up_matrix, preferred_element_type=f32)
-    sigmoid_gate = jax.nn.sigmoid(gate_linear)
-    activation = gate_linear * sigmoid_gate
-    product = activation * up_linear
-    hidden = product.astype(bf16)
-    weighted = (rows_gate * product).astype(bf16)
-    grad_down = reduced(cotangent_rows, weighted)
-    raw_back = jnp.dot(cotangent_rows, down_matrix, preferred_element_type=f32)
-    gate_grad = jnp.sum(raw_back * hidden.astype(f32), axis=1).astype(bf16)
-    scaled_back = rows_gate * raw_back
-    up_delta = (scaled_back * activation).astype(bf16)
-    gate_delta = (
-        scaled_back * up_linear * sigmoid_gate * (1.0 + gate_linear * (1.0 - sigmoid_gate))
-    ).astype(bf16)
-    grad_up = reduced(rows, up_delta)
-    grad_gate = reduced(rows, gate_delta)
-    route_back = (
-        lax.dot_general(gate_delta, gate_matrix, contract_last, preferred_element_type=f32)
-        + lax.dot_general(up_delta, up_matrix, contract_last, preferred_element_type=f32)
-    ).astype(bf16)
-    back_rows = lax.all_to_all(
-        route_back.reshape(ep, SLOTS, width), "ep", split_axis=0, concat_axis=0, tiled=True
-    )
-    router_back, grad_router = router_backward(
-        gate_grad, pick, (kernels, columns, totals, logits, marks), features, local_tokens, w_router, ep, n_dp
-    )
-
     named = jnp.any(
         assign[0][:, :, None] == jnp.arange(experts, dtype=jnp.int32), axis=1
     ).astype(bf16)
@@ -589,11 +756,41 @@
     rank = jnp.dot(earlier, named, preferred_element_type=f32)
     slot_of = jnp.where(named > 0, rank, -1.0)
     token_slots = (
-        slot_of[:, :, None] == jnp.arange(SLOTS, dtype=f32)
-    ).astype(bf16).reshape(count, experts * SLOTS)
-    expert_back = jnp.dot(token_slots, back_rows.reshape(-1, width), preferred_element_type=f32)
-    grad_tokens = (expert_back + router_back).astype(bf16)[None]
-    return grad_tokens, grad_router, grad_gate, grad_up, grad_down
+        (slot_of[:, :, None] == jnp.arange(SLOTS, dtype=f32))
+        .astype(bf16)
+        .reshape(count, experts * SLOTS)
+    )
+
+    gate_linear = jnp.dot(rows, gate_matrix, preferred_element_type=f32)
+    up_linear = jnp.dot(rows, up_matrix, preferred_element_type=f32)
+    sigmoid_gate = jax.nn.sigmoid(gate_linear)
+    activation = gate_linear * sigmoid_gate
+    product = activation * up_linear
+    hidden = product.astype(bf16)
+    weighted = (rows_gate * product).astype(bf16)
+    raw_back = jnp.dot(cotangent_rows, down_matrix, preferred_element_type=f32)
+    gate_grad = jnp.sum(raw_back * hidden.astype(f32), axis=1).astype(bf16)
+    scaled_back = rows_gate * raw_back
+    up_delta = (scaled_back * activation).astype(bf16)
+    gate_delta = (
+        scaled_back * up_linear * sigmoid_gate * (1.0 + gate_linear * (1.0 - sigmoid_gate))
+    ).astype(bf16)
+    grad_tokens, grad_router, grad_gate, grad_up, grad_down = backward(
+        gate_grad,
+        pick,
+        (kernels, columns, totals, logits, marks),
+        features,
+        local_tokens,
+        w_router,
+        rows,
+        cotangent_rows,
+        (gate_delta, up_delta, weighted),
+        token_slots,
+        (gate_matrix, up_matrix),
+        ep,
+        n_dp,
+    )
+    return grad_tokens[None], grad_router, grad_gate[None], grad_up[None], grad_down[None]
 
 
 def solution(mesh):

time: 245 us -> 206 us (0.84)
  matrix products: 42.5 us -> 9.42 us
  Pallas kernels: 151 us -> 173 us
  between operations: 14 us -> 0.76 us
  waiting for transfers between devices: 11.1 us -> 0 us
  starting transfers between devices: 6.02 us -> 0 us
    dot_general x6 -> x0, matrix products: 26.2 us -> none  [the longest x3 15.3 us: reduced(): lax.dot_general(left, right, contract_first, preferred_element_type=f32)]
    pallas_call x1, Pallas kernels: 72.3 us -> 94.1 us  [backward(): pl.pallas_call(functools.partial(backward_kernel, ep, n_dp), out_shape=(j...]
    reduce_scatter x3 -> x0, waiting for transfers between devices: 11 us -> none  [reduced(): lax.psum_scatter(product.astype(bf16), 'dp', scatter_dimension=0, tiled=T...]
    all_to_all x1 -> x0, starting transfers between devices: 5.72 us -> none  [per_device(): lax.all_to_all(route_back.reshape(ep, SLOTS, width), 'ep', split_axis=0,...]
    dot_general x1, matrix products: 6.26 us -> 1.82 us  [per_device(): up_linear = jnp.dot(rows, up_matrix, preferred_element_type=f32)]
    dot_general x1, matrix products: 7.03 us -> 3.95 us  [per_device(): gate_linear = jnp.dot(rows, gate_matrix, preferred_element_type=f32)]
    unnamed x57 -> x41, local copies, waits for them, and re-layouts: 18.3 us -> 17.5 us
  transfers between devices with their start and end apart: 4 -> 0, of which waited for: 1 -> 0; matrix products, arithmetic and copies ran while one was open for 11% -> 0% of each run, Pallas kernels for 30% -> 0%
where the time goes in v2:
time: 206 us
  Pallas kernels  173 us (84%)
  local copies, waits for them, and re-layouts  21 us (10%)
  matrix products  9.42 us (5%)
    pallas_call x1, Pallas kernels, backward(): pl.pallas_call(functools.partial(backward_kernel, ep, n_dp), out_shape=(j...  94.1 us
    pallas_call x1, Pallas kernels, dispatch(): pl.pallas_call(functools.partial(dispatch_kernel, ep), out_shape=(shape((...  78.6 us
    unnamed x41, local copies, waits for them, and re-layouts  17.5 us

profile of v2, /device:TPU:1, one launch (start us, length us, event | category | flops | bytes accessed | tf_op | source)
XLA Modules:
  0.0 205.6 jit_solution(14728151969165578434)
XLA Ops:
  0.7 0.9 copy.22
  1.8 0.7 copy.24
  2.6 0.7 eq.39
  3.2 0.8 broadcast_bitcast_fusion
  4.0 0.7 copy.25
  4.7 1.4 compare_convert_fusion.slots_ref
  6.2 2.0 copy.23.router_ref
  8.2 1.0 copy-done.1
  9.2 0.9 copy-done.9
  10.1 78.6 %shard_map.110 = (bf16[512,2048]{1,0:T(8,128)(2,1)S(1)}, bf16[512,2048]{1,0:T(8,128)(2,1)}, f32[512,1]{1,0:T(8,128)S(1)}, bf16[8,64,256]{2,1,0:T(8,128)(2,1)S(1)...) custom-call(bf16[32,2048]{1,0:T(8,128)(2,1)S(1)} %bitcast.25, ...), custom_call_target="tpu_custom_call" | custom-call | tf_op jit(solution)/shard_map/pallas_call | solution.py:306
  88.7 1.3 copy-done.2
  90.0 0.8 copy-done.5
  90.8 0.8 copy-done.6
  91.6 0.8 copy-done.7
  92.4 0.7 copy-done.8
  94.5 3.5 %fusion = f32[512,768]{1,0:T(8,128)S(1)} fusion(bf16[512,2048]{1,0:T(8,128)(2,1)} %get-tuple-element.20.cot_rows_ref, bf16[1,2048,768]{2,1,0:T(8,128)(2,1)S(1)} %copy-done), kind=kOutput, calls=%fused_computation | convolution fusion | flops 1610612736 | bytes 6815744 | tf_op jit(solution)/shard_map/dot_general | solution.py:771
  98.1 1.8 fusion.4
  100.0 4.0 %multiply_convert_fusion.2 = (bf16[512,768]{1,0:T(8,128)(2,1)}, bf16[512]{0:T(512)(128)(2,1)S(1)}, bf16[512,768]{1,0:T(8,128)(2,1)}, bf16[512,768]{1,0:T(8,128)(2,1)}) fusion(f32[512,768]{1,0:T(8,128)S(1)} %fusion.4, f32[512,768]{1,0:T(8,128)S(1)} %fusion, f32[512]{0:T(512)S(1)} %reduce, bf16[512,2048]{1,0:T(8,128)(2,1)S(1)} %copy-done.3, ...), kind=kOutput, calls=%fused_computation.4 | convolution fusion | flops 1618869760 | bytes 10750976 | tf_op jit(solution)/shard_map/dot_general | solution.py:764
  104.6 94.1 %shard_map.111 = (bf16[32,2048]{1,0:T(8,128)(2,1)}, f32[2048,64]{1,0:T(8,128)}, bf16[512,768]{1,0:T(8,128)(2,1)}, bf16[512,768]{1,0:T(8,128)(2,1)}, bf16[512,768]{1,0:T(8,128)(2,1)}) custom-call(bf16[8,512]{1,0:T(8,128)(2,1)} %broadcast_in_dim.14.grad_ref, bf16[8,64,256]{2,1,0:T(8,128)(2,1)} %copy-done.8, f32[4,64,2048]{2,1,0:T(8,128)} %get-tuple-element.23.kernels, ...), custom_call_target="tpu_custom_call" | custom-call | tf_op jit(solution)/shard_map/pallas_call | solution.py:683
  198.7 2.4 %copy.27 = f32[2048,64]{0,1:T(8,128)} copy(f32[2048,64]{1,0:T(8,128)} %get-tuple-element.46) | data formatting | bytes 1048576
  201.0 0.7 copy.32
  201.7 2.1 %copy.33 = bf16[1,512,768]{2,1,0:T(8,128)(2,1)} copy(bf16[1,512,768]{2,1,0:T(8,128)(2,1)} %bitcast.33) | data formatting | bytes 1572864
  203.8 0.9 copy.34
  204.7 0.9 copy.35
  (32 shorter events, 2.4 us)
Async XLA Ops:
  0.6 93.9 %copy-start = (bf16[1,2048,768]{2,1,0:T(8,128)(2,1)S(1)}, bf16[1,2048,768]{2,1,0:T(8,128)(2,1)}, u32[]{:S(2)}) copy-start(bf16[1,2048,768]{2,1,0:T(8,128)(2,1)} %param.13) | copy-start | bytes 9437188
  0.6 7.5 %copy-start.4 = (bf16[1,32,2048]{2,1,0:T(8,128)(2,1)S(1)}, bf16[1,32,2048]{2,1,0:T(8,128)(2,1)}, u32[]{:S(2)}) copy-start(bf16[1,32,2048]{2,1,0:T(8,128)(2,1)} %param.7) | copy-start | bytes 393220
  8.2 1.0 copy-start.1
  9.2 0.9 copy-start.9
  88.7 1.3 copy-start.2
  90.0 0.8 copy-start.5
  90.8 0.8 copy-start.6
  91.6 0.8 copy-start.7
  92.4 0.7 copy-start.8
  93.1 0.6 copy-start.10
  93.8 0.6 copy-start.11
  94.5 3.6 %copy-start.3 = (bf16[512,2048]{1,0:T(8,128)(2,1)S(1)}, bf16[512,2048]{1,0:T(8,128)(2,1)}, u32[]{:S(2)}) copy-start(bf16[512,2048]{1,0:T(8,128)(2,1)} %copy-done.2) | copy-start | bytes 6291460
  94.5 3.6 %copy-start.12 = (bf16[1,2048,768]{2,1,0:T(8,128)(2,1)S(1)}, bf16[1,2048,768]{2,1,0:T(8,128)(2,1)}, u32[]{:S(2)}) copy-start(bf16[1,2048,768]{2,1,0:T(8,128)(2,1)} %param.12) | copy-start | bytes 9437188
  98.1 1.9 copy-start.13
  198.6 2.4 %copy-start.16 = (bf16[32,2048]{1,0:T(8,128)(2,1)S(1)}, bf16[32,2048]{1,0:T(8,128)(2,1)}, u32[]{:S(2)}) copy-start(bf16[32,2048]{1,0:T(8,128)(2,1)} %get-tuple-element.30) | copy-start | bytes 393220
  201.0 2.8 %copy-start.15 = (bf16[512,768]{1,0:T(8,128)(2,1)S(1)}, bf16[512,768]{1,0:T(8,128)(2,1)}, u32[]{:S(2)}) copy-start(bf16[512,768]{1,0:T(8,128)(2,1)} %get-tuple-element.33) | copy-start | bytes 2359300
  201.7 3.0 %copy-start.14 = (bf16[512,768]{1,0:T(8,128)(2,1)S(1)}, bf16[512,768]{1,0:T(8,128)(2,1)}, u32[]{:S(2)}) copy-start(bf16[512,768]{1,0:T(8,128)(2,1)} %get-tuple-element.34) | copy-start | bytes 2359300

commit v3 on v2

v3 whole, which is shorter than its diff:
```python
import functools
import heapq

import jax
import jax.numpy as jnp
from jax import lax
from jax.experimental import pallas as pl
from jax.experimental.pallas import tpu as pltpu
from jax.sharding import PartitionSpec as P

ITERS = 3
SLOTS = 8
LANES = 128
GROUP = 256
MESH = pl.DeviceIdType.MESH
f32 = jnp.float32
bf16 = jnp.bfloat16

cos_scale = 48.0
eps_norm = 1e-06
contract_first = (((0,), (0,)), ((), ()))
contract_last = (((1,), (1,)), ((), ()))


def torus_of(ep):
    ny = max(1, min(4, ep // 4))
    return ny, ep // (2 * ny)


def gather_plan(ny, nz, unit_us, hop_us=1.0):
    def half(part, side):
        return side if part is None else (part if part == side else -1)

    def spread(which, a, b, part):
        na, nb = (nz, ny) if which % 2 == 0 else (ny, nz)
        out = []

        def along(axis, n, at, signs):
            for sign in signs:
                last = abs(at) + 1 == n // 2
                piece = half(part, 0 if sign > 0 else 1) if last else part
                if piece != -1:
                    out.append((axis, sign, piece))

        def onward(at, n):
            if n == 1:
                return ()
            if at == 0:
                return (1, -1)
            return ((1,) if at > 0 else (-1,)) if abs(at) < n // 2 else ()

        if b == 0:
            along(0, na, a, onward(a, na))
        along(1, nb, b, onward(b, nb))
        return out

    heap, order, free, steps, ids = [], 0, {}, [], 0
    for which in range(len(unit_us)):
        heapq.heappush(heap, (0.0, order, None, which, 0, 0, None))
        order += 1
    while heap:
        now, _, arrival, which, a, b, part = heapq.heappop(heap)
        dy, dz = (b, a) if which % 2 == 0 else (a, b)
        sends = []
        for axis, sign, piece in spread(which, a, b, part):
            link = "zy"[axis] if which % 2 == 0 else "yz"[axis]
            share = 1.0 if piece is None else 0.5
            end = max(now, free.get((link, sign), 0.0)) + unit_us[which] * share
            free[(link, sign)] = end
            na, nb = (a + sign, b) if axis == 0 else (a, b + sign)
            heapq.heappush(heap, (end + hop_us, order, ids, which, na, nb, piece))
            sends.append((ids, which, dy, dz, part if piece is None else piece, link, sign))
            order += 1
            ids += 1
        sends.append((ids, which, dy, dz, part, "mate", 0))
        ids += 1
        steps.append((None if arrival is None else (arrival, which, dy, dz, part), sends))
    return steps, ids


def pieces_of(width):
    extra = max(LANES, width * 3 // 16 // LANES * LANES)
    return ((0, 0, width), (1, extra, width - extra), (1, 0, extra))


def unit_times(width):
    return tuple(2.8 * columns / width for _, _, columns in pieces_of(width))


def place(ep, ny, nz):
    me = lax.axis_index("ep")
    core = lax.rem(me, 2)
    chip = me // 2
    return me, core, chip // nz, lax.rem(chip, nz)


def at_ep(nz, y, z, core):
    return (y * nz + z) * 2 + core


def split_three(value):
    high = value.astype(bf16)
    rest = value - high.astype(f32)
    middle = rest.astype(bf16)
    return high, middle, (rest - middle.astype(f32)).astype(bf16)


def balance(meta, kernels, columns, totals, logits, marks, per_group):
    experts, total = logits.shape
    for g in range(total // GROUP):
        blocks = [meta[b % 2, b // 2] for b in range(g * per_group, (g + 1) * per_group)]
        flipped = jnp.concatenate(blocks, axis=0).T
        logits[:, g * GROUP : (g + 1) * GROUP] = flipped[:experts]
        marks[:, g * GROUP : (g + 1) * GROUP] = flipped[experts:]
    kernels[0] = jnp.exp(logits[...])
    for s in range(ITERS):
        kernel = kernels[s]
        column = jnp.sum(kernel, axis=1, keepdims=True)
        scaled = kernel / column
        row = jnp.sum(scaled, axis=0, keepdims=True)
        kernels[s + 1] = scaled / row
        columns[s] = jnp.broadcast_to(column, (experts, LANES))
        totals[s : s + 1, :] = row
    picked = jnp.where(marks[...] > 0.0, kernels[ITERS], 0.0)
    totals[ITERS : ITERS + 1, :] = jnp.sum(picked, axis=0, keepdims=True)
    totals[ITERS + 1 : ITERS + 2, :] = jnp.max(marks[...], axis=0, keepdims=True)


def moe_kernel(
    ep,
    n_dp,
    tok_ref,
    cot_ref,
    assign_ref,
    router_ref,
    w_gate_hbm,
    w_up_hbm,
    w_down_hbm,
    tokens_out,
    router_out,
    gate_out,
    up_out,
    down_out,
    tok_all,
    cot_all,
    meta,
    rows_tok,
    rows_cot,
    rows_gate,
    gate_grad,
    gate_delta,
    up_delta,
    weighted_rows,
    w_gate,
    w_up,
    w_down,
    row_mask,
    row_gate,
    pick,
    kernels,
    columns,
    totals,
    logits_all,
    marks,
    features_ref,
    slots_ref,
    table,
    grad,
    spread,
    turned,
    parts,
    shares,
    route_back,
    back_rows,
    got_far,
    got_near,
    meta_send,
    meta_recv,
    block_sends,
    block_recvs,
    sends,
    recvs,
    row_sends,
    row_recvs,
    far_sends,
    far_recvs,
    near_sends,
    near_recvs,
    weight_sems,
):
    ny, nz = torus_of(ep)
    count, width = tok_ref.shape
    experts = router_ref.shape[1]
    hidden_units = gate_delta.shape[1]
    total = ep * count
    groups = total // GROUP
    per_group = GROUP // count
    slots = per_group * SLOTS
    n_shares = width // LANES
    repeat = ep // n_shares
    chunk = width // n_dp // 2
    chunk_blocks = chunk // count
    ring = n_dp == 4
    dp = lax.axis_index("dp")
    me, core, y, z = place(ep, ny, nz)
    mine = y * nz + z
    mate = (dp, at_ep(nz, y, z, 1 - core))
    z_peers = [(dp, at_ep(nz, y, lax.rem(z + k, nz), core)) for k in range(1, nz)]
    y_peers = [(dp, at_ep(nz, lax.rem(y + k, ny), z, core)) for k in range(1, ny)]
    x_peers = [(lax.rem(dp + k, n_dp), me) for k in range(1, n_dp)]
    right, left = (lax.rem(dp + 1, n_dp), me), (lax.rem(dp + n_dp - 1, n_dp), me)
    share, twin = me // repeat, lax.rem(me, repeat)
    share_peers = [
        (dp, lax.rem(share + k, n_shares) * repeat + twin) for k in range(1, n_shares)
    ]

    barrier = pltpu.get_barrier_semaphore()

    def greet(k, carry):
        pl.semaphore_signal(
            barrier, inc=1, device_id=(dp, lax.rem(me + k, ep)), device_id_type=MESH
        )
        return carry

    lax.fori_loop(1, ep, greet, 0)
    for peer in x_peers:
        pl.semaphore_signal(barrier, inc=1, device_id=peer, device_id_type=MESH)
    fetches = [
        pltpu.make_async_copy(source, target, weight_sems.at[k])
        for k, (source, target) in enumerate(
            ((w_gate_hbm, w_gate), (w_up_hbm, w_up), (w_down_hbm, w_down))
        )
    ]
    for fetch in fetches:
        fetch.start()

    local = tok_ref[...]
    router = router_ref[...]
    tok_all[me] = local
    cot_all[me] = cot_ref[...]
    wide = local.astype(f32)
    inverse_local = 1.0 / jnp.sqrt(jnp.sum(wide * wide, axis=1, keepdims=True) + eps_norm)
    router_wide = router.astype(f32)
    square_row = jnp.sum(router_wide * router_wide, axis=0, keepdims=True) + eps_norm
    inner = jnp.dot(local, router, preferred_element_type=f32)
    logits = cos_scale * inner * inverse_local / jnp.sqrt(square_row)
    ids = lax.broadcasted_iota(jnp.int32, (count, experts), 1)
    routes = assign_ref[...]
    hit = jnp.zeros((count, experts), f32)
    for k in range(routes.shape[1]):
        hit = jnp.where(routes[:, k : k + 1] == ids, inverse_local, hit)
    meta[core, mine] = jnp.concatenate([logits, hit], axis=1)

    pl.semaphore_wait(barrier, ep - 1 + n_dp - 1)

    def meta_copy(n, block, blocks, peer, c=core):
        ref = meta.at[c, pl.ds(block, blocks)]
        return pltpu.make_async_remote_copy(
            src_ref=ref, dst_ref=ref, send_sem=meta_send.at[n], recv_sem=meta_recv.at[n],
            device_id=peer, device_id_type=MESH,
        )

    meta_copies = [meta_copy(k, mine, 1, p) for k, p in enumerate(z_peers)]
    for copy in meta_copies:
        copy.start()

    ends = {
        ("z", 1): (dp, at_ep(nz, y, lax.rem(z + 1, nz), core)),
        ("z", -1): (dp, at_ep(nz, y, lax.rem(z + nz - 1, nz), core)),
        ("y", 1): (dp, at_ep(nz, lax.rem(y + 1, ny), z, core)),
        ("y", -1): (dp, at_ep(nz, lax.rem(y + ny - 1, ny), z, core)),
        ("mate", 0): mate,
    }

    def view(which, dy, dz, part, c):
        block = at_ep(nz, lax.rem(y - dy + 2 * ny, ny), lax.rem(z - dz + 2 * nz, nz), c)
        first, rows = (0, count) if part is None else (part * (count // 2), count // 2)
        ref, column, columns_held = pieces_of(width)[which]
        held = (tok_all, cot_all)[ref]
        return held.at[block, pl.ds(first, rows), pl.ds(column, columns_held)]

    def block_copy(n, ref, end):
        return pltpu.make_async_remote_copy(
            src_ref=ref, dst_ref=ref, send_sem=block_sends.at[n], recv_sem=block_recvs.at[n],
            device_id=ends[end], device_id_type=MESH,
        )

    gather_copies, mate_arrivals = [], []

    def run(step):
        arrival, step_sends = step
        if arrival is not None:
            n, which, dy, dz, part = arrival
            block_copy(n, view(which, dy, dz, part, core), ("z", 1)).wait_recv()
        for n, which, dy, dz, part, link, sign in step_sends:
            copy = block_copy(n, view(which, dy, dz, part, core), (link, sign))
            copy.start()
            gather_copies.append(copy)
            if link == "mate":
                mate_arrivals.append((n, which, dy, dz, part))

    steps = gather_plan(ny, nz, unit_times(width))[0]
    first, second = len(steps) // 12, len(steps) // 6
    third, fourth = len(steps) // 4, len(steps) // 3
    for at, step in enumerate(steps):
        if at == first:
            for k in range(nz - 1):
                meta_copy(k, y * nz + lax.rem(z - 1 - k + nz, nz), 1, mate).wait_recv()
            for k, peer in enumerate(y_peers):
                meta_copies.append(meta_copy(nz - 1 + k, y * nz, nz, peer))
                meta_copies[-1].start()
        if at == second:
            for k in range(ny - 1):
                block = lax.rem(y - 1 - k + ny, ny) * nz
                meta_copy(nz - 1 + k, block, nz, mate).wait_recv()
            meta_copies.append(meta_copy(nz + ny - 2, 0, ny * nz, mate))
            meta_copies[-1].start()
        if at == third:
            meta_copy(nz + ny - 2, 0, ny * nz, mate, 1 - core).wait_recv()
            named = jnp.where(hit > 0.0, 1.0, 0.0)
            tokens_down = lax.broadcasted_iota(jnp.int32, (count, count), 0)
            tokens_across = lax.broadcasted_iota(jnp.int32, (count, count), 1)
            sooner = jnp.where(tokens_across < tokens_down, 1.0, 0.0).astype(bf16)
            rank = jnp.dot(sooner, named.astype(bf16), preferred_element_type=f32)
            slot_of = jnp.where(named > 0.0, rank, -1.0).astype(bf16)
            expert_down = lax.broadcasted_iota(jnp.int32, (experts, experts * SLOTS), 0)
            slot_across = lax.broadcasted_iota(jnp.int32, (experts, experts * SLOTS), 1)
            widen = jnp.where(slot_across // SLOTS == expert_down, 1.0, 0.0).astype(bf16)
            slot_wide = jnp.dot(slot_of, widen, preferred_element_type=f32)
            across = lax.broadcasted_iota(jnp.int32, (count, experts * SLOTS), 1)
            slots_ref[...] = jnp.where(
                slot_wide == lax.rem(across, SLOTS).astype(f32), 1.0, 0.0
            ).astype(bf16)
        if at == fourth:
            balance(meta, kernels, columns, totals, logits_all, marks, per_group)
            held = marks[pl.ds(me, 1), :] > 0.0
            kernel = jnp.where(held, kernels[ITERS, pl.ds(me, 1), :], 0.0)
            row_mask[...] = jnp.where(held, 1.0, 0.0)
            row_gate[...] = (kernel / totals[ITERS : ITERS + 1, :]).astype(bf16).astype(f32)
            before = lax.broadcasted_iota(jnp.int32, (GROUP, GROUP), 0)
            after = lax.broadcasted_iota(jnp.int32, (GROUP, GROUP), 1)
            earlier = jnp.where(
                (before < after) & (before // count == after // count), 1.0, 0.0
            ).astype(bf16)
            slot_ids = lax.broadcasted_iota(jnp.int32, (slots, GROUP), 0).astype(f32)
            base = (lax.broadcasted_iota(jnp.int32, (1, GROUP), 1) // count * SLOTS).astype(f32)
            for g in range(groups):
                mask = row_mask[:, g * GROUP : (g + 1) * GROUP]
                place_in = jnp.dot(
                    jnp.broadcast_to(mask, (8, GROUP)).astype(bf16), earlier,
                    preferred_element_type=f32,
                )[0:1]
                target = jnp.where(mask > 0.0, base + place_in, -1.0)
                chosen = jnp.where(slot_ids == target, 1.0, 0.0)
                rows_gate[g * slots : (g + 1) * slots, :] = jnp.sum(
                    chosen * row_gate[:, g * GROUP : (g + 1) * GROUP], axis=1, keepdims=True
                )
                pick[g] = chosen.astype(bf16)
        run(step)
    for n, which, dy, dz, part in mate_arrivals:
        block_copy(n, view(which, dy, dz, part, 1 - core), ("mate", 0)).wait_recv()

    def compact(g, carry):
        rows = pl.ds(pl.multiple_of(g * slots, slots), slots)
        blocks = pl.ds(g * per_group, per_group)
        rows_tok[rows, :] = jnp.dot(
            pick[g], tok_all[blocks].reshape(GROUP, width), preferred_element_type=f32
        ).astype(bf16)
        rows_cot[rows, :] = jnp.dot(
            pick[g], cot_all[blocks].reshape(GROUP, width), preferred_element_type=f32
        ).astype(bf16)
        return carry

    lax.fori_loop(0, groups, compact, 0)
    for fetch in fetches:
        fetch.wait()

    gate_grad[...] = jnp.zeros_like(gate_grad)
    row_step = min(256, ep * SLOTS)
    unit_step = min(256, hidden_units)
    row_steps = ep * SLOTS // row_step

    def expert(i, carry):
        rows = pl.ds(pl.multiple_of(lax.rem(i, row_steps) * row_step, row_step), row_step)
        units = pl.ds(pl.multiple_of(i // row_steps * unit_step, unit_step), unit_step)
        gate_linear = jnp.dot(rows_tok[rows, :], w_gate[:, units], preferred_element_type=f32)
        up_linear = jnp.dot(rows_tok[rows, :], w_up[:, units], preferred_element_type=f32)
        raw_back = jnp.dot(rows_cot[rows, :], w_down[:, units], preferred_element_type=f32)
        sigmoid_gate = jax.nn.sigmoid(gate_linear)
        activation = gate_linear * sigmoid_gate
        product = activation * up_linear
        gate = rows_gate[rows, :]
        weighted_rows[rows, units] = (gate * product).astype(bf16)
        gate_grad[rows, :] += jnp.sum(
            raw_back * product.astype(bf16).astype(f32), axis=1, keepdims=True
        )
        scaled_back = gate * raw_back
        up_delta[rows, units] = (scaled_back * activation).astype(bf16)
        gate_delta[rows, units] = (
            scaled_back * up_linear * sigmoid_gate * (1.0 + gate_linear * (1.0 - sigmoid_gate))
        ).astype(bf16)
        return carry

    lax.fori_loop(0, row_steps * (hidden_units // unit_step), expert, 0)
    features_ref[...] = tok_all[:, :, pl.ds(pl.multiple_of(share * LANES, LANES), LANES)]
    for copy in [*meta_copies, *gather_copies]:
        copy.wait_send()

    started = []
    across_table = width // hidden_units

    def buffer(n):
        held = (tok_all, cot_all)[n % 2]
        block, column = n // 2 // across_table, n // 2 % across_table
        return held.at[
            pl.ds(block * chunk_blocks, chunk_blocks),
            :,
            pl.ds(column * hidden_units, hidden_units),
        ]

    def far_buffer(a, side):
        return buffer(a * 2 + side)

    def near_buffer(a, side, half):
        return buffer(6 + a * 4 + side * 2 + half)

    def copy_of(n, ref, peer):
        return pltpu.make_async_remote_copy(
            src_ref=ref, dst_ref=ref, send_sem=sends.at[n], recv_sem=recvs.at[n],
            device_id=peer, device_id_type=MESH,
        )

    def start(copy):
        copy.start()
        started.append(copy)

    def far_copy(a, side):
        return pltpu.make_async_remote_copy(
            src_ref=far_buffer(a, side), dst_ref=got_far.at[a, side],
            send_sem=far_sends.at[a, side], recv_sem=far_recvs.at[a, side],
            device_id=(right, left)[side], device_id_type=MESH,
        )

    def near_copy(a, side, half):
        return pltpu.make_async_remote_copy(
            src_ref=near_buffer(a, side, half), dst_ref=got_near.at[a, side, half],
            send_sem=near_sends.at[a, side, half], recv_sem=near_recvs.at[a, side, half],
            device_id=(right, left)[side], device_id_type=MESH,
        )

    pairs = ((rows_cot, weighted_rows), (rows_tok, up_delta), (rows_tok, gate_delta))
    outs = (down_out, up_out, gate_out)
    arrays = range(3)

    def gradient(a, away, half):
        block = lax.rem(dp + away, n_dp)
        start_row = pl.multiple_of(block * (2 * chunk) + half * chunk, chunk)
        left_rows, right_rows = pairs[a]
        return lax.dot_general(
            left_rows[:, pl.ds(start_row, chunk)], right_rows[...], contract_first,
            preferred_element_type=f32,
        )

    def put(ref, value):
        ref[...] = value.astype(bf16).reshape(chunk_blocks, count, hidden_units)

    def far(a):
        for side in range(2):
            put(far_buffer(a, side), gradient(a, 2, side))
            start(far_copy(a, side))

    def near_plain(a):
        for side in range(2):
            put(near_buffer(a, side, 1 - side), gradient(a, (1, n_dp - 1)[side], 1 - side))
            start(near_copy(a, side, 1 - side))

    def near_joined(a):
        for side in range(2):
            mixed = gradient(a, (1, n_dp - 1)[side], side)
            far_copy(a, side).wait_recv()
            put(
                near_buffer(a, side, side),
                mixed + got_far[a, side].reshape(chunk, hidden_units).astype(f32),
            )
            start(near_copy(a, side, side))

    if ring:
        far(0)

    for g in range(groups):
        held = gate_grad[g * slots : (g + 1) * slots, :].astype(bf16).astype(f32)
        table[mine, core, g : g + 1, :] = jnp.sum(
            held * pick[g].astype(f32), axis=0, keepdims=True
        )
    n = 0

    def part(chip, chips):
        return table.at[pl.ds(chip, chips)]

    start(copy_of(n, table.at[mine, core], mate))
    if ring:
        far(1)
    copy_of(n, table.at[mine, 1 - core], mate).wait_recv()
    n += 1
    for k, peer in enumerate(z_peers):
        start(copy_of(n + k, part(mine, 1), peer))
    if ring:
        far(2)
    for k in range(nz - 1):
        copy_of(n + k, part(y * nz + lax.rem(z - 1 - k + nz, nz), 1), mate).wait_recv()
    n += nz - 1
    for k, peer in enumerate(y_peers):
        start(copy_of(n + k, part(y * nz, nz), peer))

    pieces = 4
    rows_each = ep // pieces

    def rows_back(q, carry):
        rows = pl.ds(pl.multiple_of(q * rows_each * SLOTS, rows_each * SLOTS), rows_each * SLOTS)
        value = lax.dot_general(
            gate_delta[rows, :], w_gate[...], contract_last, preferred_element_type=f32
        ) + lax.dot_general(up_delta[rows, :], w_up[...], contract_last, preferred_element_type=f32)
        route_back[pl.ds(q * rows_each, rows_each)] = value.astype(bf16).reshape(
            rows_each, SLOTS, width
        )
        return carry

    lax.fori_loop(0, pieces, rows_back, 0)

    def row_copy(k, from_block, to_block, peer):
        return pltpu.make_async_remote_copy(
            src_ref=route_back.at[from_block], dst_ref=back_rows.at[to_block],
            send_sem=row_sends.at[k], recv_sem=row_recvs.at[k],
            device_id=(dp, peer), device_id_type=MESH,
        )

    def send_rows(k, carry):
        peer = lax.rem(me + k, ep)
        row_copy(k, peer, me, peer).start()
        return carry

    lax.fori_loop(1, ep, send_rows, 0)
    back_rows[me] = route_back[me]

    for k in range(ny - 1):
        copy_of(n + k, part(lax.rem(y - 1 - k + ny, ny) * nz, nz), mate).wait_recv()
    n += ny - 1

    for g in range(groups):
        both = table[:, :, g, :]
        grad[:, g * GROUP : (g + 1) * GROUP] = both.reshape(experts, GROUP)
    inverse_token = totals[ITERS + 1 : ITERS + 2, :]
    picked_sum = totals[ITERS : ITERS + 1, :]
    member = marks[...] > 0.0
    route = jnp.where(member, grad[...], 0.0)
    gates = jnp.where(member, kernels[ITERS], 0.0) / picked_sum
    grad[...] = jnp.where(
        member, (route - jnp.sum(route * gates, axis=0, keepdims=True)) / picked_sum, 0.0
    )
    for s in reversed(range(ITERS)):
        kernel = kernels[s + 1]
        row = totals[s : s + 1, :]
        column = columns[s][:, 0:1]
        slope = grad[...]
        slope = (slope - jnp.sum(slope * kernel, axis=0, keepdims=True)) / row
        moment = jnp.sum(slope * (kernel * row), axis=1, keepdims=True)
        grad[...] = (slope - moment) / column
    logit_grad = grad[...] * kernels[0]
    weighted = logit_grad * logits_all[...]
    square = jnp.broadcast_to(square_row, (LANES, experts)).T[:, 0:1]
    turn = logit_grad * (cos_scale * inverse_token) / jnp.sqrt(square)
    spread[:experts, :] = turn
    spread[experts:, :] = jnp.broadcast_to(
        jnp.sum(weighted, axis=0, keepdims=True) * inverse_token * inverse_token,
        (spread.shape[0] - experts, total),
    )

    features = features_ref[...].reshape(total, LANES)
    product = jnp.dot(
        jnp.concatenate(split_three(turn), axis=0), features, preferred_element_type=f32
    )
    product = product[:experts] + product[experts : 2 * experts] + product[2 * experts :]
    own_router = router_ref[pl.ds(pl.multiple_of(share * LANES, LANES), LANES), :].astype(f32).T
    parts[dp] = product - own_router * (jnp.sum(weighted, axis=1, keepdims=True) / square)
    for k, peer in enumerate(x_peers):
        start(copy_of(n + k, parts.at[dp], peer))

    if ring:
        for a in arrays:
            near_plain(a)
        for a in arrays:
            near_joined(a)

    turned[...] = spread[:, pl.ds(pl.multiple_of(me * count // LANES * LANES, LANES), LANES)].T
    own = turned[pl.ds(pl.multiple_of(lax.rem(me, LANES // count) * count, count), count), :]
    back = jnp.zeros((count, width), f32)
    for term in split_three(own[:, :experts]):
        back += lax.dot_general(term, router, contract_last, preferred_element_type=f32)
    back -= tok_ref[...].astype(f32) * own[:, experts : experts + 1]

    for k in range(n_dp - 1):
        copy_of(n + k, parts.at[lax.rem(dp - 1 - k + n_dp, n_dp)], mate).wait_recv()
    n += n_dp - 1
    summed = parts[0]
    for k in range(1, n_dp):
        summed += parts[k]
    shares[share] = summed
    for k, peer in enumerate(share_peers):
        start(copy_of(n + k, shares.at[share], peer))

    def got_rows(k, carry):
        block = lax.rem(me - k + ep, ep)
        row_copy(k, block, block, block).wait_recv()
        return carry

    lax.fori_loop(1, ep, got_rows, 0)
    tokens_out[...] = (
        back
        + jnp.dot(
            slots_ref[...], back_rows[...].reshape(ep * SLOTS, width), preferred_element_type=f32
        )
    ).astype(bf16)

    for k in range(n_shares - 1):
        copy_of(n + k, shares.at[lax.rem(share - 1 - k + n_shares, n_shares)], mate).wait_recv()
    router_out[...] = shares[...]

    def finish(a, half):
        value = gradient(a, 0, half)
        if ring:
            for side in range(2):
                near_copy(a, side, half).wait_recv()
                value += got_near[a, side, half].reshape(chunk, hidden_units).astype(f32)
        outs[a][half * chunk : (half + 1) * chunk, :] = value.astype(bf16)

    for a in arrays:
        for half in range(2):
            finish(a, half)

    def sent_rows(k, carry):
        peer = lax.rem(me + k, ep)
        row_copy(k, peer, me, peer).wait_send()
        return carry

    lax.fori_loop(1, ep, sent_rows, 0)
    for copy in started:
        copy.wait_send()


def per_device(ep, n_dp, tokens, cotangent, assign, w_router, w_gate, w_up, w_down):
    ny, nz = torus_of(ep)
    _, count, width = tokens.shape
    experts = w_router.shape[1]
    hidden_units = w_gate.shape[2]
    total = ep * count
    groups = total // GROUP
    n_shares = width // LANES
    rows = ep * SLOTS
    chunk = width // n_dp // 2
    copies = 1 + nz - 1 + ny - 1 + n_dp - 1 + n_shares - 1
    blocks = gather_plan(ny, nz, unit_times(width))[1]
    shape, vmem_array, dma = jax.ShapeDtypeStruct, pltpu.VMEM, pltpu.SemaphoreType.DMA
    vmem = pl.BlockSpec(memory_space=pltpu.VMEM)
    anywhere = pl.BlockSpec(memory_space=pl.ANY)
    gradient = shape((2 * chunk, hidden_units), bf16)
    small = nz + ny - 1
    grad_tokens, shares, grad_gate, grad_up, grad_down = pl.pallas_call(
        functools.partial(moe_kernel, ep, n_dp),
        out_shape=(
            shape((count, width), bf16),
            shape((n_shares, experts, LANES), f32),
            gradient,
            gradient,
            gradient,
        ),
        in_specs=[vmem] * 4 + [anywhere] * 3,
        out_specs=(vmem,) * 5,
        scratch_shapes=[
            vmem_array((ep, count, width), bf16),
            vmem_array((ep, count, width), bf16),
            vmem_array((2, ny * nz, count, 2 * experts), f32),
            vmem_array((rows, width), bf16),
            vmem_array((rows, width), bf16),
            vmem_array((rows, 1), f32),
            vmem_array((rows, 1), f32),
            vmem_array((rows, hidden_units), bf16),
            vmem_array((rows, hidden_units), bf16),
            vmem_array((rows, hidden_units), bf16),
            vmem_array((width, hidden_units), bf16),
            vmem_array((width, hidden_units), bf16),
            vmem_array((width, hidden_units), bf16),
            vmem_array((1, total), f32),
            vmem_array((1, total), f32),
            vmem_array((groups, GROUP // count * SLOTS, GROUP), bf16),
            vmem_array((ITERS + 1, experts, total), f32),
            vmem_array((ITERS, experts, LANES), f32),
            vmem_array((8, total), f32),
            vmem_array((experts, total), f32),
            vmem_array((experts, total), f32),
            vmem_array((ep, count, LANES), bf16),
            vmem_array((count, experts * SLOTS), bf16),
            vmem_array((ny * nz, 2, groups, GROUP), f32),
            vmem_array((experts, total), f32),
            vmem_array((LANES, total), f32),
            vmem_array((LANES, LANES), f32),
            vmem_array((n_dp, experts, LANES), f32),
            vmem_array((n_shares, experts, LANES), f32),
            vmem_array((ep, SLOTS, width), bf16),
            vmem_array((ep, SLOTS, width), bf16),
            vmem_array((3, 2, chunk // count, count, hidden_units), bf16),
            vmem_array((3, 2, 2, chunk // count, count, hidden_units), bf16),
            dma((small,)),
            dma((small,)),
            dma((blocks,)),
            dma((blocks,)),
            dma((copies,)),
            dma((copies,)),
            dma((ep,)),
            dma((ep,)),
            dma((3, 2)),
            dma((3, 2)),
            dma((3, 2, 2)),
            dma((3, 2, 2)),
            dma((3,)),
        ],
        compiler_params=pltpu.CompilerParams(
            collective_id=1, has_side_effects=True, vmem_limit_bytes=60 * 2**20
        ),
    )(tokens[0], cotangent[0], assign[0], w_router, w_gate[0], w_up[0], w_down[0])
    grad_router = shares.transpose(0, 2, 1).reshape(width, experts)
    return grad_tokens[None], grad_router, grad_gate[None], grad_up[None], grad_down[None]


def solution(mesh):
    return jax.shard_map(
        functools.partial(per_device, mesh.shape["ep"], mesh.shape["dp"]),
        mesh=mesh,
        in_specs=(
            P("dp", "ep", None),
            P("dp", "ep", None),
            P("dp", "ep", None),
            P(),
            P("ep", None, None),
            P("ep", None, None),
            P("ep", None, None),
        ),
        out_specs=(
            P("dp", "ep", None),
            P(),
            P("ep", "dp", None),
            P("ep", "dp", None),
            P("ep", "dp", None),
        ),
        check_vma=False,
    )
```

time: 206 us -> 183 us (0.89)
  local copies, waits for them, and re-layouts: 21 us -> 10.7 us
  matrix products: 9.42 us -> 0 us
    dot_general x4 -> x0, matrix products: 9.42 us -> none  [the longest x1 3.95 us: per_device(): gate_linear = jnp.dot(rows, gate_matrix, preferred_element_type=f32)]
    unnamed x41 -> x10, local copies, waits for them, and re-layouts: 17.5 us -> 8.72 us
    eq x4 -> x0, local copies, waits for them, and re-layouts: 2.19 us -> none  [per_device(): slot_of[:, :, None] == jnp.arange(SLOTS, dtype=f32)]
    pallas_call x2 -> x1, Pallas kernels: 173 us -> 171 us  [per_device(): pl.pallas_call(functools.partial(moe_kernel, ep, n_dp), out_shape=(shape(...]
where the time goes in v3:
time: 183 us; the launch traced here: 182 us
  Pallas kernels  171 us (93%)
  local copies, waits for them, and re-layouts  10.7 us (6%)
    pallas_call x1, Pallas kernels, per_device(): pl.pallas_call(functools.partial(moe_kernel, ep, n_dp), out_shape=(shape(...  171 us
    unnamed x10, local copies, waits for them, and re-layouts  8.72 us

profile of v3, /device:TPU:1, one launch (start us, length us, event | category | flops | bytes accessed | tf_op | source)
XLA Modules:
  0.0 182.4 jit_solution(2950987961476530592)
XLA Ops:
  0.6 1.4 copy.14
  2.0 2.0 %copy.15.router_ref = bf16[2048,64]{1,0:T(8,128)(2,1)} copy(bf16[2048,64]{0,1:T(8,128)(2,1)} %param.10) | data formatting | bytes 524288 | tf_op args[3]
  4.0 171.0 %shard_map.110 = (bf16[32,2048]{1,0:T(8,128)(2,1)}, f32[16,64,128]{2,1,0:T(8,128)}, bf16[512,768]{1,0:T(8,128)(2,1)}, bf16[512,768]{1,0:T(8,128)(2,1)}, bf16[512,768]{1,0:T(8,128)(2,1)}) custom-call(bf16[32,2048]{1,0:T(8,128)(2,1)} %bitcast.22, bf16[32,2048]{1,0:T(8,128)(2,1)} %bitcast.23, s32[32,8]{1,0:T(8,128)} %bitcast.25, ...), custom_call_target="tpu_custom_call" | custom-call | tf_op jit(solution)/shard_map/pallas_call | solution.py:667
  175.0 0.0 copy-start.1
  175.0 0.0 copy-start
  175.0 2.0 %copy_bitcast_fusion = f32[2048,64]{0,1:T(8,128)} fusion(f32[16,64,128]{2,1,0:T(8,128)} %get-tuple-element.11), kind=kLoop, calls=%fused_computation | loop fusion | bytes 1048576 | tf_op jit(solution)/shard_map/reshape | solution.py:730
  177.0 1.6 copy.23
  178.5 2.1 %copy.24 = bf16[1,512,768]{2,1,0:T(8,128)(2,1)} copy(bf16[1,512,768]{2,1,0:T(8,128)(2,1)} %bitcast.21) | data formatting | bytes 1572864
  180.6 0.0 copy-done.1
  180.6 0.9 copy.25
  181.5 0.0 copy-done
  181.5 0.9 copy.26
Async XLA Ops:
  175.0 5.6 %copy-start.1 = (bf16[512,768]{1,0:T(8,128)(2,1)S(1)}, bf16[512,768]{1,0:T(8,128)(2,1)}, u32[]{:S(2)}) copy-start(bf16[512,768]{1,0:T(8,128)(2,1)} %get-tuple-element.13) | copy-start | bytes 2359300
  175.0 6.5 %copy-start = (bf16[512,768]{1,0:T(8,128)(2,1)S(1)}, bf16[512,768]{1,0:T(8,128)(2,1)}, u32[]{:S(2)}) copy-start(bf16[512,768]{1,0:T(8,128)(2,1)} %get-tuple-element.14) | copy-start | bytes 2359300

commit v4 on v3

--- a/solution.py
+++ b/solution.py
@@ -27,7 +27,7 @@
     return ny, ep // (2 * ny)
 
 
-def gather_plan(ny, nz, unit_us, hop_us=1.0):
+def gather_plan(ny, nz, unit_us, begin_us, hop_us=1.0):
     def half(part, side):
         return side if part is None else (part if part == side else -1)
 
@@ -56,7 +56,7 @@
 
     heap, order, free, steps, ids = [], 0, {}, [], 0
     for which in range(len(unit_us)):
-        heapq.heappush(heap, (0.0, order, None, which, 0, 0, None))
+        heapq.heappush(heap, (begin_us[which], order, None, which, 0, 0, None))
         order += 1
     while heap:
         now, _, arrival, which, a, b, part = heapq.heappop(heap)
@@ -79,12 +79,17 @@
 
 
 def pieces_of(width):
-    extra = max(LANES, width * 3 // 16 // LANES * LANES)
-    return ((0, 0, width), (1, extra, width - extra), (1, 0, extra))
-
-
-def unit_times(width):
-    return tuple(2.8 * columns / width for _, _, columns in pieces_of(width))
+    split = width * 5 // 8 // LANES * LANES
+    return tuple(
+        (held, column, columns)
+        for held in (0, 1)
+        for column, columns in ((0, split), (split, width - split))
+    )
+
+
+def plan_of(ny, nz, width):
+    times = tuple(2.8 * columns / width for _, _, columns in pieces_of(width))
+    return gather_plan(ny, nz, times, (0.0, 0.0, 4.0, 4.0))
 
 
 def place(ep, ny, nz):
@@ -105,14 +110,16 @@
     return high, middle, (rest - middle.astype(f32)).astype(bf16)
 
 
-def balance(meta, kernels, columns, totals, logits, marks, per_group):
-    experts, total = logits.shape
+def balance(meta, kernels, columns, totals, marks, per_group):
+    experts, total = marks.shape
     for g in range(total // GROUP):
-        blocks = [meta[b % 2, b // 2] for b in range(g * per_group, (g + 1) * per_group)]
+        blocks = []
+        for b in range(g * per_group, (g + 1) * per_group):
+            block = meta[b % 2, b // 2]
+            blocks += [block[:, :experts], block[:, experts:]]
         flipped = jnp.concatenate(blocks, axis=0).T
-        logits[:, g * GROUP : (g + 1) * GROUP] = flipped[:experts]
-        marks[:, g * GROUP : (g + 1) * GROUP] = flipped[experts:]
-    kernels[0] = jnp.exp(logits[...])
+        marks[:, g * GROUP : (g + 1) * GROUP] = flipped
+    kernels[0] = jnp.abs(marks[...])
     for s in range(ITERS):
         kernel = kernels[s]
         column = jnp.sum(kernel, axis=1, keepdims=True)
@@ -121,9 +128,8 @@
         kernels[s + 1] = scaled / row
         columns[s] = jnp.broadcast_to(column, (experts, LANES))
         totals[s : s + 1, :] = row
-    picked = jnp.where(marks[...] > 0.0, kernels[ITERS], 0.0)
+    picked = jnp.where(marks[...] < 0.0, kernels[ITERS], 0.0)
     totals[ITERS : ITERS + 1, :] = jnp.sum(picked, axis=0, keepdims=True)
-    totals[ITERS + 1 : ITERS + 2, :] = jnp.max(marks[...], axis=0, keepdims=True)
 
 
 def moe_kernel(
@@ -160,10 +166,11 @@
     kernels,
     columns,
     totals,
-    logits_all,
     marks,
-    features_ref,
     slots_ref,
+    gate_all,
+    up_all,
+    spare,
     table,
     grad,
     spread,
@@ -190,7 +197,7 @@
 ):
     ny, nz = torus_of(ep)
     count, width = tok_ref.shape
-    experts = router_ref.shape[1]
+    experts = router_ref.shape[0]
     hidden_units = gate_delta.shape[1]
     total = ep * count
     groups = total // GROUP
@@ -241,15 +248,18 @@
     wide = local.astype(f32)
     inverse_local = 1.0 / jnp.sqrt(jnp.sum(wide * wide, axis=1, keepdims=True) + eps_norm)
     router_wide = router.astype(f32)
-    square_row = jnp.sum(router_wide * router_wide, axis=0, keepdims=True) + eps_norm
-    inner = jnp.dot(local, router, preferred_element_type=f32)
+    square = jnp.sum(router_wide * router_wide, axis=1, keepdims=True) + eps_norm
+    square_row = jnp.broadcast_to(square, (experts, LANES)).T[0:1, :]
+    inner = lax.dot_general(local, router, contract_last, preferred_element_type=f32)
     logits = cos_scale * inner * inverse_local / jnp.sqrt(square_row)
-    ids = lax.broadcasted_iota(jnp.int32, (count, experts), 1)
-    routes = assign_ref[...]
-    hit = jnp.zeros((count, experts), f32)
+    ids = lax.broadcasted_iota(jnp.int32, (count, experts), 1).astype(f32)
+    routes = assign_ref[...].astype(f32).T
+    named = jnp.zeros((count, experts), f32)
     for k in range(routes.shape[1]):
-        hit = jnp.where(routes[:, k : k + 1] == ids, inverse_local, hit)
-    meta[core, mine] = jnp.concatenate([logits, hit], axis=1)
+        named = jnp.where(routes[:, k : k + 1] == ids, 1.0, named)
+    start_kernel = jnp.exp(logits)
+    signed = jnp.where(named > 0.0, -start_kernel, start_kernel)
+    meta[core, mine] = jnp.concatenate([signed[: count // 2], signed[count // 2 :]], axis=1)
 
     pl.semaphore_wait(barrier, ep - 1 + n_dp - 1)
 
@@ -299,9 +309,58 @@
             if link == "mate":
                 mate_arrivals.append((n, which, dy, dz, part))
 
-    steps = gather_plan(ny, nz, unit_times(width))[0]
-    first, second = len(steps) // 12, len(steps) // 6
-    third, fourth = len(steps) // 4, len(steps) // 3
+    steps = plan_of(ny, nz, width)[0]
+
+    def compact(held, rows_ref, g):
+        blocks = held[g * per_group : (g + 1) * per_group].reshape(GROUP, width)
+        rows_ref[g * slots : (g + 1) * slots, :] = jnp.dot(
+            pick[g], blocks, preferred_element_type=f32
+        ).astype(bf16)
+
+    row_step = min(256, ep * SLOTS)
+    unit_step = min(256, hidden_units)
+    row_steps = ep * SLOTS // row_step
+    expert_steps = row_steps * (hidden_units // unit_step)
+
+    def tile(i):
+        row, unit = i % row_steps * row_step, i // row_steps * unit_step
+        return slice(row, row + row_step), slice(unit, unit + unit_step)
+
+    def forward(i):
+        rows, units = tile(i)
+        gate_linear = jnp.dot(rows_tok[rows, :], w_gate[:, units], preferred_element_type=f32)
+        up_linear = jnp.dot(rows_tok[rows, :], w_up[:, units], preferred_element_type=f32)
+        gate_all[rows, units] = gate_linear
+        up_all[rows, units] = up_linear
+        product = gate_linear * jax.nn.sigmoid(gate_linear) * up_linear
+        weighted_rows[rows, units] = (rows_gate[rows, :] * product).astype(bf16)
+
+    def norms(g):
+        values = tok_all[g * per_group : (g + 1) * per_group].reshape(GROUP, width).astype(f32)
+        inverse = 1.0 / jnp.sqrt(jnp.sum(values * values, axis=1, keepdims=True) + eps_norm)
+        totals[ITERS + 1 : ITERS + 2, g * GROUP : (g + 1) * GROUP] = jnp.broadcast_to(
+            inverse, (GROUP, LANES)
+        ).T[0:1, :]
+
+    def mates(wanted):
+        for n, which, dy, dz, part in mate_arrivals:
+            if pieces_of(width)[which][0] == wanted:
+                block_copy(n, view(which, dy, dz, part, 1 - core), ("mate", 0)).wait_recv()
+
+    def fetched():
+        for fetch in fetches:
+            fetch.wait()
+
+    token_work = [functools.partial(compact, tok_all, rows_tok, g) for g in range(groups)]
+    token_work += [fetched]
+    token_work += [functools.partial(forward, i) for i in range(expert_steps)]
+    token_work += [functools.partial(norms, g) for g in range(groups)]
+    tokens_in = max(
+        at for at, step in enumerate(steps) if pieces_of(width)[step[0][1] if step[0] else 0][0] == 0
+    )
+    first, second = tokens_in // 6, tokens_in // 3
+    third, fourth = tokens_in // 2, tokens_in * 2 // 3
+    ready = min(tokens_in + 4, len(steps) - 1)
     for at, step in enumerate(steps):
         if at == first:
             for k in range(nz - 1):
@@ -317,7 +376,6 @@
             meta_copies[-1].start()
         if at == third:
             meta_copy(nz + ny - 2, 0, ny * nz, mate, 1 - core).wait_recv()
-            named = jnp.where(hit > 0.0, 1.0, 0.0)
             tokens_down = lax.broadcasted_iota(jnp.int32, (count, count), 0)
             tokens_across = lax.broadcasted_iota(jnp.int32, (count, count), 1)
             sooner = jnp.where(tokens_across < tokens_down, 1.0, 0.0).astype(bf16)
@@ -332,8 +390,8 @@
                 slot_wide == lax.rem(across, SLOTS).astype(f32), 1.0, 0.0
             ).astype(bf16)
         if at == fourth:
-            balance(meta, kernels, columns, totals, logits_all, marks, per_group)
-            held = marks[pl.ds(me, 1), :] > 0.0
+            balance(meta, kernels, columns, totals, marks, per_group)
+            held = marks[pl.ds(me, 1), :] < 0.0
             kernel = jnp.where(held, kernels[ITERS, pl.ds(me, 1), :], 0.0)
             row_mask[...] = jnp.where(held, 1.0, 0.0)
             row_gate[...] = (kernel / totals[ITERS : ITERS + 1, :]).astype(bf16).astype(f32)
@@ -356,63 +414,28 @@
                     chosen * row_gate[:, g * GROUP : (g + 1) * GROUP], axis=1, keepdims=True
                 )
                 pick[g] = chosen.astype(bf16)
+        if at == ready:
+            mates(0)
+        if at > ready:
+            share_of = -(-len(token_work) // max(1, len(steps) - at))
+            for work in token_work[:share_of]:
+                work()
+            token_work = token_work[share_of:]
         run(step)
-    for n, which, dy, dz, part in mate_arrivals:
-        block_copy(n, view(which, dy, dz, part, 1 - core), ("mate", 0)).wait_recv()
-
-    def compact(g, carry):
-        rows = pl.ds(pl.multiple_of(g * slots, slots), slots)
-        blocks = pl.ds(g * per_group, per_group)
-        rows_tok[rows, :] = jnp.dot(
-            pick[g], tok_all[blocks].reshape(GROUP, width), preferred_element_type=f32
-        ).astype(bf16)
-        rows_cot[rows, :] = jnp.dot(
-            pick[g], cot_all[blocks].reshape(GROUP, width), preferred_element_type=f32
-        ).astype(bf16)
-        return carry
-
-    lax.fori_loop(0, groups, compact, 0)
-    for fetch in fetches:
-        fetch.wait()
-
-    gate_grad[...] = jnp.zeros_like(gate_grad)
-    row_step = min(256, ep * SLOTS)
-    unit_step = min(256, hidden_units)
-    row_steps = ep * SLOTS // row_step
-
-    def expert(i, carry):
-        rows = pl.ds(pl.multiple_of(lax.rem(i, row_steps) * row_step, row_step), row_step)
-        units = pl.ds(pl.multiple_of(i // row_steps * unit_step, unit_step), unit_step)
-        gate_linear = jnp.dot(rows_tok[rows, :], w_gate[:, units], preferred_element_type=f32)
-        up_linear = jnp.dot(rows_tok[rows, :], w_up[:, units], preferred_element_type=f32)
-        raw_back = jnp.dot(rows_cot[rows, :], w_down[:, units], preferred_element_type=f32)
-        sigmoid_gate = jax.nn.sigmoid(gate_linear)
-        activation = gate_linear * sigmoid_gate
-        product = activation * up_linear
-        gate = rows_gate[rows, :]
-        weighted_rows[rows, units] = (gate * product).astype(bf16)
-        gate_grad[rows, :] += jnp.sum(
-            raw_back * product.astype(bf16).astype(f32), axis=1, keepdims=True
-        )
-        scaled_back = gate * raw_back
-        up_delta[rows, units] = (scaled_back * activation).astype(bf16)
-        gate_delta[rows, units] = (
-            scaled_back * up_linear * sigmoid_gate * (1.0 + gate_linear * (1.0 - sigmoid_gate))
-        ).astype(bf16)
-        return carry
-
-    lax.fori_loop(0, row_steps * (hidden_units // unit_step), expert, 0)
-    features_ref[...] = tok_all[:, :, pl.ds(pl.multiple_of(share * LANES, LANES), LANES)]
-    for copy in [*meta_copies, *gather_copies]:
-        copy.wait_send()
+    for work in token_work:
+        work()
+    mates(1)
+    for g in range(groups):
+        compact(cot_all, rows_cot, g)
 
     started = []
     across_table = width // hidden_units
 
     def buffer(n):
-        held = (tok_all, cot_all)[n % 2]
-        block, column = n // 2 // across_table, n // 2 % across_table
-        return held.at[
+        if n < 2:
+            return spare.at[n]
+        block, column = (n - 2) // across_table, (n - 2) % across_table
+        return cot_all.at[
             pl.ds(block * chunk_blocks, chunk_blocks),
             :,
             pl.ds(column * hidden_units, hidden_units),
@@ -486,6 +509,31 @@
 
     if ring:
         far(0)
+
+    gate_grad[...] = jnp.zeros_like(gate_grad)
+
+    def expert(i, carry):
+        rows = pl.ds(pl.multiple_of(lax.rem(i, row_steps) * row_step, row_step), row_step)
+        units = pl.ds(pl.multiple_of(i // row_steps * unit_step, unit_step), unit_step)
+        raw_back = jnp.dot(rows_cot[rows, :], w_down[:, units], preferred_element_type=f32)
+        gate_linear = gate_all[rows, units]
+        up_linear = up_all[rows, units]
+        sigmoid_gate = jax.nn.sigmoid(gate_linear)
+        activation = gate_linear * sigmoid_gate
+        product = activation * up_linear
+        gate_grad[rows, :] += jnp.sum(
+            raw_back * product.astype(bf16).astype(f32), axis=1, keepdims=True
+        )
+        scaled_back = rows_gate[rows, :] * raw_back
+        up_delta[rows, units] = (scaled_back * activation).astype(bf16)
+        gate_delta[rows, units] = (
+            scaled_back * up_linear * sigmoid_gate * (1.0 + gate_linear * (1.0 - sigmoid_gate))
+        ).astype(bf16)
+        return carry
+
+    lax.fori_loop(0, expert_steps, expert, 0)
+    for copy in [*meta_copies, *gather_copies]:
+        copy.wait_send()
 
     for g in range(groups):
         held = gate_grad[g * slots : (g + 1) * slots, :].astype(bf16).astype(f32)
@@ -551,7 +599,7 @@
         grad[:, g * GROUP : (g + 1) * GROUP] = both.reshape(experts, GROUP)
     inverse_token = totals[ITERS + 1 : ITERS + 2, :]
     picked_sum = totals[ITERS : ITERS + 1, :]
-    member = marks[...] > 0.0
+    member = marks[...] < 0.0
     route = jnp.where(member, grad[...], 0.0)
     gates = jnp.where(member, kernels[ITERS], 0.0) / picked_sum
     grad[...] = jnp.where(
@@ -566,8 +614,7 @@
         moment = jnp.sum(slope * (kernel * row), axis=1, keepdims=True)
         grad[...] = (slope - moment) / column
     logit_grad = grad[...] * kernels[0]
-    weighted = logit_grad * logits_all[...]
-    square = jnp.broadcast_to(square_row, (LANES, experts)).T[:, 0:1]
+    weighted = logit_grad * jnp.log(kernels[0])
     turn = logit_grad * (cos_scale * inverse_token) / jnp.sqrt(square)
     spread[:experts, :] = turn
     spread[experts:, :] = jnp.broadcast_to(
@@ -575,12 +622,13 @@
         (spread.shape[0] - experts, total),
     )
 
-    features = features_ref[...].reshape(total, LANES)
+    own_lanes = pl.ds(pl.multiple_of(share * LANES, LANES), LANES)
+    features = tok_all[:, :, own_lanes].reshape(total, LANES)
     product = jnp.dot(
         jnp.concatenate(split_three(turn), axis=0), features, preferred_element_type=f32
     )
     product = product[:experts] + product[experts : 2 * experts] + product[2 * experts :]
-    own_router = router_ref[pl.ds(pl.multiple_of(share * LANES, LANES), LANES), :].astype(f32).T
+    own_router = router_ref[:, own_lanes].astype(f32)
     parts[dp] = product - own_router * (jnp.sum(weighted, axis=1, keepdims=True) / square)
     for k, peer in enumerate(x_peers):
         start(copy_of(n + k, parts.at[dp], peer))
@@ -595,7 +643,7 @@
     own = turned[pl.ds(pl.multiple_of(lax.rem(me, LANES // count) * count, count), count), :]
     back = jnp.zeros((count, width), f32)
     for term in split_three(own[:, :experts]):
-        back += lax.dot_general(term, router, contract_last, preferred_element_type=f32)
+        back += jnp.dot(term, router, preferred_element_type=f32)
     back -= tok_ref[...].astype(f32) * own[:, experts : experts + 1]
 
     for k in range(n_dp - 1):
@@ -623,7 +671,8 @@
 
     for k in range(n_shares - 1):
         copy_of(n + k, shares.at[lax.rem(share - 1 - k + n_shares, n_shares)], mate).wait_recv()
-    router_out[...] = shares[...]
+    for k in range(n_shares):
+        router_out[:, k * LANES : (k + 1) * LANES] = shares[k]
 
     def finish(a, half):
         value = gradient(a, 0, half)
@@ -645,6 +694,35 @@
     lax.fori_loop(1, ep, sent_rows, 0)
     for copy in started:
         copy.wait_send()
+
+
+def copy_kernel(*refs):
+    arrays = (len(refs) - 2) // 3
+    sources, targets, stages = (refs[k * arrays : (k + 1) * arrays] for k in range(3))
+    ins = [pltpu.make_async_copy(a, b, refs[-2].at[k]) for k, (a, b) in enumerate(zip(sources, stages))]
+    outs = [pltpu.make_async_copy(a, b, refs[-1].at[k]) for k, (a, b) in enumerate(zip(stages, targets))]
+    for copy in ins:
+        copy.start()
+    for arrived, copy in zip(ins, outs):
+        arrived.wait()
+        copy.start()
+    for copy in outs:
+        copy.wait()
+
+
+def handed_on(arrays):
+    anywhere = pl.BlockSpec(memory_space=pl.ANY)
+    return pl.pallas_call(
+        copy_kernel,
+        out_shape=tuple(jax.ShapeDtypeStruct(a.shape, a.dtype) for a in arrays),
+        in_specs=[anywhere] * len(arrays),
+        out_specs=(anywhere,) * len(arrays),
+        scratch_shapes=[
+            *(pltpu.VMEM(a.shape, a.dtype) for a in arrays),
+            pltpu.SemaphoreType.DMA((len(arrays),)),
+            pltpu.SemaphoreType.DMA((len(arrays),)),
+        ],
+    )(*arrays)
 
 
 def per_device(ep, n_dp, tokens, cotangent, assign, w_router, w_gate, w_up, w_down):
@@ -658,17 +736,17 @@
     rows = ep * SLOTS
     chunk = width // n_dp // 2
     copies = 1 + nz - 1 + ny - 1 + n_dp - 1 + n_shares - 1
-    blocks = gather_plan(ny, nz, unit_times(width))[1]
+    blocks = plan_of(ny, nz, width)[1]
     shape, vmem_array, dma = jax.ShapeDtypeStruct, pltpu.VMEM, pltpu.SemaphoreType.DMA
     vmem = pl.BlockSpec(memory_space=pltpu.VMEM)
     anywhere = pl.BlockSpec(memory_space=pl.ANY)
     gradient = shape((2 * chunk, hidden_units), bf16)
     small = nz + ny - 1
-    grad_tokens, shares, grad_gate, grad_up, grad_down = pl.pallas_call(
+    outs = pl.pallas_call(
         functools.partial(moe_kernel, ep, n_dp),
         out_shape=(
             shape((count, width), bf16),
-            shape((n_shares, experts, LANES), f32),
+            shape((experts, width), f32),
             gradient,
             gradient,
             gradient,
@@ -678,7 +756,7 @@
         scratch_shapes=[
             vmem_array((ep, count, width), bf16),
             vmem_array((ep, count, width), bf16),
-            vmem_array((2, ny * nz, count, 2 * experts), f32),
+            vmem_array((2, ny * nz, count // 2, 2 * experts), f32),
             vmem_array((rows, width), bf16),
             vmem_array((rows, width), bf16),
             vmem_array((rows, 1), f32),
@@ -696,9 +774,10 @@
             vmem_array((ITERS, experts, LANES), f32),
             vmem_array((8, total), f32),
             vmem_array((experts, total), f32),
-            vmem_array((experts, total), f32),
-            vmem_array((ep, count, LANES), bf16),
             vmem_array((count, experts * SLOTS), bf16),
+            vmem_array((rows, hidden_units), f32),
+            vmem_array((rows, hidden_units), f32),
+            vmem_array((2, chunk // count, count, hidden_units), bf16),
             vmem_array((ny * nz, 2, groups, GROUP), f32),
             vmem_array((experts, total), f32),
             vmem_array((LANES, total), f32),
@@ -726,9 +805,9 @@
         compiler_params=pltpu.CompilerParams(
             collective_id=1, has_side_effects=True, vmem_limit_bytes=60 * 2**20
         ),
-    )(tokens[0], cotangent[0], assign[0], w_router, w_gate[0], w_up[0], w_down[0])
-    grad_router = shares.transpose(0, 2, 1).reshape(width, experts)
-    return grad_tokens[None], grad_router, grad_gate[None], grad_up[None], grad_down[None]
+    )(tokens[0], cotangent[0], assign[0].T, w_router.T, w_gate[0], w_up[0], w_down[0])
+    grad_tokens, grad_router, grad_gate, grad_up, grad_down = handed_on(outs)
+    return grad_tokens[None], grad_router.T, grad_gate[None], grad_up[None], grad_down[None]
 
 
 def solution(mesh):

time: 183 us -> 170 us (0.929)
  local copies, waits for them, and re-layouts: 10.7 us -> 0 us
  Pallas kernels: 171 us -> 169 us
    unnamed x10 -> x0, local copies, waits for them, and re-layouts: 8.72 us -> none
    pallas_call x1, Pallas kernels: 171 us -> 166 us  [per_device(): pl.pallas_call(functools.partial(moe_kernel, ep, n_dp), out_shape=(shape(...]
    pallas_call x0 -> x1, Pallas kernels: none -> 2.85 us  [handed_on(): pl.pallas_call(copy_kernel, out_shape=tuple((jax.ShapeDtypeStruct(a.shape...]
    reshape x1 -> x0, local copies, waits for them, and re-layouts: 1.98 us -> none  [per_device(): grad_router = shares.transpose(0, 2, 1).reshape(width, experts)]
where the time goes in v4:
time: 170 us
  Pallas kernels  169 us (99%)
    pallas_call x1, Pallas kernels, per_device(): pl.pallas_call(functools.partial(moe_kernel, ep, n_dp), out_shape=(shape(...  166 us

profile of v4, /device:TPU:1, one launch (start us, length us, event | category | flops | bytes accessed | tf_op | source)
XLA Modules:
  0.0 169.9 jit_solution(4210846461143615597)
XLA Ops:
  0.6 166.2 %shard_map.110 = (bf16[32,2048]{1,0:T(8,128)(2,1)}, f32[64,2048]{1,0:T(8,128)}, bf16[512,768]{1,0:T(8,128)(2,1)}, bf16[512,768]{1,0:T(8,128)(2,1)}, bf16[512,768]{1,0:T(8,128)(2,1)}) custom-call(bf16[32,2048]{1,0:T(8,128)(2,1)} %bitcast.18, bf16[32,2048]{1,0:T(8,128)(2,1)} %bitcast.19, s32[8,32]{1,0:T(8,128)} %bitcast.20, bf16[64,2048]{1,0:T(8,128)(2,1)} %bitcast.17, ...), custom_call_target="tpu_custom_call" | custom-call | tf_op jit(solution)/shard_map/pallas_call | solution.py:745
  166.8 2.9 %shard_map.111 = (bf16[32,2048]{1,0:T(8,128)(2,1)}, f32[64,2048]{1,0:T(8,128)}, bf16[512,768]{1,0:T(8,128)(2,1)}, bf16[512,768]{1,0:T(8,128)(2,1)}, bf16[512,768]{1,0:T(8,128)(2,1)}) custom-call(bf16[32,2048]{1,0:T(8,128)(2,1)} %get-tuple-element.15.refs_0_, f32[64,2048]{1,0:T(8,128)} %get-tuple-element.16.refs_1_, ...), custom_call_target="tpu_custom_call" | custom-call | tf_op jit(solution)/shard_map/pallas_call | solution.py:715

commit v5 on v4

--- a/solution.py
+++ b/solution.py
@@ -89,7 +89,7 @@
 
 def plan_of(ny, nz, width):
     times = tuple(2.8 * columns / width for _, _, columns in pieces_of(width))
-    return gather_plan(ny, nz, times, (0.0, 0.0, 4.0, 4.0))
+    return gather_plan(ny, nz, times, (0.0, 0.0, 14.0, 14.0))
 
 
 def place(ep, ny, nz):
@@ -355,6 +355,7 @@
     token_work += [fetched]
     token_work += [functools.partial(forward, i) for i in range(expert_steps)]
     token_work += [functools.partial(norms, g) for g in range(groups)]
+    all_work = len(token_work)
     tokens_in = max(
         at for at, step in enumerate(steps) if pieces_of(width)[step[0][1] if step[0] else 0][0] == 0
     )
@@ -417,10 +418,11 @@
         if at == ready:
             mates(0)
         if at > ready:
-            share_of = -(-len(token_work) // max(1, len(steps) - at))
-            for work in token_work[:share_of]:
+            done = all_work - len(token_work)
+            due = all_work * (at - ready) // (len(steps) - 1 - ready) - done
+            for work in token_work[:due]:
                 work()
-            token_work = token_work[share_of:]
+            token_work = token_work[due:]
         run(step)
     for work in token_work:
         work()
@@ -589,6 +591,8 @@
 
     lax.fori_loop(1, ep, send_rows, 0)
     back_rows[me] = route_back[me]
+    if ring:
+        near_plain(0)
 
     for k in range(ny - 1):
         copy_of(n + k, part(lax.rem(y - 1 - k + ny, ny) * nz, nz), mate).wait_recv()
@@ -634,7 +638,7 @@
         start(copy_of(n + k, parts.at[dp], peer))
 
     if ring:
-        for a in arrays:
+        for a in (1, 2):
             near_plain(a)
         for a in arrays:
             near_joined(a)

time: 170 us -> 168 us (0.988)
  Pallas kernels: 169 us -> 166 us
    pallas_call x1, Pallas kernels: 166 us -> 163 us  [per_device(): pl.pallas_call(functools.partial(moe_kernel, ep, n_dp), out_shape=(shape(...]
where the time goes in v5:
time: 168 us; the launch traced here: 167 us
  Pallas kernels  166 us (99%)
    pallas_call x1, Pallas kernels, per_device(): pl.pallas_call(functools.partial(moe_kernel, ep, n_dp), out_shape=(shape(...  163 us

profile of v5, /device:TPU:1, one launch (start us, length us, event | category | flops | bytes accessed | tf_op | source)
XLA Modules:
  0.0 166.6 jit_solution(11249133793022918808)
XLA Ops:
  0.6 163.0 %shard_map.110 = (bf16[32,2048]{1,0:T(8,128)(2,1)}, f32[64,2048]{1,0:T(8,128)}, bf16[512,768]{1,0:T(8,128)(2,1)}, bf16[512,768]{1,0:T(8,128)(2,1)}, bf16[512,768]{1,0:T(8,128)(2,1)}) custom-call(bf16[32,2048]{1,0:T(8,128)(2,1)} %bitcast.18, bf16[32,2048]{1,0:T(8,128)(2,1)} %bitcast.19, s32[8,32]{1,0:T(8,128)} %bitcast.20, bf16[64,2048]{1,0:T(8,128)(2,1)} %bitcast.17, ...), custom_call_target="tpu_custom_call" | custom-call | tf_op jit(solution)/shard_map/pallas_call | solution.py:749
  163.6 2.9 %shard_map.111 = (bf16[32,2048]{1,0:T(8,128)(2,1)}, f32[64,2048]{1,0:T(8,128)}, bf16[512,768]{1,0:T(8,128)(2,1)}, bf16[512,768]{1,0:T(8,128)(2,1)}, bf16[512,768]{1,0:T(8,128)(2,1)}) custom-call(bf16[32,2048]{1,0:T(8,128)(2,1)} %get-tuple-element.15.refs_0_, f32[64,2048]{1,0:T(8,128)} %get-tuple-element.16.refs_1_, ...), custom_call_target="tpu_custom_call" | custom-call | tf_op jit(solution)/shard_map/pallas_call | solution.py:719

commit v6 on v5

--- a/solution.py
+++ b/solution.py
@@ -171,6 +171,7 @@
     gate_all,
     up_all,
     spare,
+    staged,
     table,
     grad,
     spread,
@@ -194,6 +195,7 @@
     near_sends,
     near_recvs,
     weight_sems,
+    out_sems,
 ):
     ny, nz = torus_of(ep)
     count, width = tok_ref.shape
@@ -684,11 +686,14 @@
             for side in range(2):
                 near_copy(a, side, half).wait_recv()
                 value += got_near[a, side, half].reshape(chunk, hidden_units).astype(f32)
-        outs[a][half * chunk : (half + 1) * chunk, :] = value.astype(bf16)
-
-    for a in arrays:
-        for half in range(2):
-            finish(a, half)
+        staged[a, half] = value.astype(bf16)
+        copy = pltpu.make_async_copy(
+            staged.at[a, half], outs[a].at[pl.ds(half * chunk, chunk)], out_sems.at[a, half]
+        )
+        copy.start()
+        return copy
+
+    written = [finish(a, half) for a in arrays for half in range(2)]
 
     def sent_rows(k, carry):
         peer = lax.rem(me + k, ep)
@@ -698,6 +703,8 @@
     lax.fori_loop(1, ep, sent_rows, 0)
     for copy in started:
         copy.wait_send()
+    for copy in written:
+        copy.wait()
 
 
 def copy_kernel(*refs):
@@ -756,7 +763,7 @@
             gradient,
         ),
         in_specs=[vmem] * 4 + [anywhere] * 3,
-        out_specs=(vmem,) * 5,
+        out_specs=(vmem, vmem, anywhere, anywhere, anywhere),
         scratch_shapes=[
             vmem_array((ep, count, width), bf16),
             vmem_array((ep, count, width), bf16),
@@ -782,6 +789,7 @@
             vmem_array((rows, hidden_units), f32),
             vmem_array((rows, hidden_units), f32),
             vmem_array((2, chunk // count, count, hidden_units), bf16),
+            vmem_array((3, 2, chunk, hidden_units), bf16),
             vmem_array((ny * nz, 2, groups, GROUP), f32),
             vmem_array((experts, total), f32),
             vmem_array((LANES, total), f32),
@@ -805,6 +813,7 @@
             dma((3, 2, 2)),
             dma((3, 2, 2)),
             dma((3,)),
+            dma((3, 2)),
         ],
         compiler_params=pltpu.CompilerParams(
             collective_id=1, has_side_effects=True, vmem_limit_bytes=60 * 2**20

time: 168 us -> 168 us (level)
  no operation moved by 1% of the time
where the time goes in v6:
time: 168 us; the launch traced here: 166 us
  Pallas kernels  165 us (98%)
    pallas_call x1, Pallas kernels, per_device(): pl.pallas_call(functools.partial(moe_kernel, ep, n_dp), out_shape=(shape(...  162 us

profile of v6, /device:TPU:1, one launch (start us, length us, event | category | flops | bytes accessed | tf_op | source)
XLA Modules:
  0.0 166.2 jit_solution(5552460819228910483)
XLA Ops:
  0.6 162.5 %shard_map.110 = (bf16[32,2048]{1,0:T(8,128)(2,1)}, f32[64,2048]{1,0:T(8,128)}, bf16[512,768]{1,0:T(8,128)(2,1)}, bf16[512,768]{1,0:T(8,128)(2,1)}, bf16[512,768]{1,0:T(8,128)(2,1)}) custom-call(bf16[32,2048]{1,0:T(8,128)(2,1)} %bitcast.18, bf16[32,2048]{1,0:T(8,128)(2,1)} %bitcast.19, s32[8,32]{1,0:T(8,128)} %bitcast.20, bf16[64,2048]{1,0:T(8,128)(2,1)} %bitcast.17, ...), custom_call_target="tpu_custom_call" | custom-call | tf_op jit(solution)/shard_map/pallas_call | solution.py:756
  163.1 2.9 %shard_map.111 = (bf16[32,2048]{1,0:T(8,128)(2,1)}, f32[64,2048]{1,0:T(8,128)}, bf16[512,768]{1,0:T(8,128)(2,1)}, bf16[512,768]{1,0:T(8,128)(2,1)}, bf16[512,768]{1,0:T(8,128)(2,1)}) custom-call(bf16[32,2048]{1,0:T(8,128)(2,1)} %get-tuple-element.15.refs_0_, f32[64,2048]{1,0:T(8,128)} %get-tuple-element.16.refs_1_, ...), custom_call_target="tpu_custom_call" | custom-call | tf_op jit(solution)/shard_map/pallas_call | solution.py:726
